TPU v7x, 32 devices: a whole 2x2x4 slice. The times are simulated.
32 devices in a mesh: corpus: 8 (over z, y), query: 4 (over x, core).
Axes of the slice: x: 2, y: 2, z: 4, core: 2. Of those that a mesh axis runs over, the one named last changes fastest.
Arguments:
- queries: bfloat16 [8192, 768], P(('corpus', 'query')), may hold values from -8 to 8
- probes: int32 [8192, 4], P(('corpus', 'query')), may hold values from 0 to 255, as said below
- targets: int32 [8192, 8], P(('corpus', 'query')), may hold values from 0 to 4095, all different within a row
- passage_codes: int32 [256, 96, 1024], P('corpus'), may hold values from 0 to 15
- codebook: float32 [16, 768], replicated, may hold values from -6 to 6
Outputs:
- grad_queries: bfloat16 [8192, 768], P(('corpus', 'query'))
- codebook_step: float32 [16, 768], replicated
Inputs may be any that keep to these rules, and one draw needn't show every extreme that they name: `probes`: each row names 4 different lists; list l belongs to index l // 32 of corpus. In every aligned block of 256 rows (the rows of one device) no list is named more than 8 times, and one list, the same one in every block, is named exactly 8 times. `targets`: each row names 8 different candidates; column r holds the candidate of rank r.
All inputs are finite; a program needn't handle non-finite values.
Results may differ from a plain program's by a relative error of at most 0.01.
The roundings to bfloat16 on the way count: a program that leaves them out, or rounds other values in their place, can miss the bound.
Values may be sent and summed in bfloat16 or wider, within the bound.
A program may use at most 192 MiB of HBM per device.

v0:
```python
import jax
import jax.numpy as jnp
from jax import lax
from jax.sharding import PartitionSpec as P

D = 768
SUBSPACES = 96
CENTROIDS = 16
SUBDIM = 8
PASSAGES = 1024
PROBES = 4
TARGETS = 8


NEGATIVE = -1e30
EPSILON = 1e-06


def rank_weights():
    levels = jnp.arange(TARGETS, dtype=jnp.int32).astype(jnp.float32)
    return 2.0 * (TARGETS - levels) / (TARGETS * (TARGETS + 1.0))


def rank_slots(list_keys, key_count, keep):
    key_ids = jnp.arange(key_count, dtype=jnp.int32)
    marked = ((list_keys[:, None] == key_ids[None, :]) & keep[:, None]).astype(jnp.int32)
    running = jnp.cumsum(marked, axis=0)
    return jnp.sum(marked * running, axis=1) - 1


def note_block(probes, targets):
    row_count = probes.shape[0]
    probe_cols = jnp.arange(PROBES, dtype=jnp.int32)
    inside = targets[:, None, :] // PASSAGES == probe_cols[None, :, None]
    target_spot = jnp.where(inside, targets[:, None, :] % PASSAGES, -1)
    query_ids = jnp.broadcast_to(
        jnp.arange(row_count, dtype=jnp.int32)[:, None, None], (row_count, PROBES, 1)
    )
    return jnp.concatenate([query_ids, target_spot], axis=2).reshape(
        row_count * PROBES, TARGETS + 1
    )


def lookup_rows(rows_block, codebook):
    lead_shape = rows_block.shape[:-1]
    split_rows = rows_block.astype(jnp.float32).reshape(lead_shape + (SUBSPACES, SUBDIM))
    centroids = codebook.reshape(CENTROIDS, SUBSPACES, SUBDIM)
    lut_rows = jnp.einsum(
        "...me,kme->...mk", split_rows, centroids, precision=lax.Precision.HIGHEST
    )
    return lut_rows.reshape(lead_shape + (SUBSPACES * CENTROIDS,)).astype(jnp.bfloat16)


def code_one_hot(code_block):
    levels = jnp.arange(CENTROIDS, dtype=jnp.int32)
    marked = code_block[:, :, None, :] == levels[None, None, :, None]
    return marked.astype(jnp.bfloat16).reshape(
        code_block.shape[0], SUBSPACES * CENTROIDS, code_block.shape[2]
    )


def group_size(lists_dev, slot_rows):
    group_width = 1
    while (
        group_width * 2 <= lists_dev
        and lists_dev % (group_width * 2) == 0
        and (group_width * slot_rows < 512)
    ):
        group_width = group_width * 2
    return group_width


def first_pass(got_rows, passage_codes, codebook, group_width):
    lists_dev, slot_rows = (got_rows.shape[0], got_rows.shape[1])
    groups = lists_dev // group_width

    def score_piece(pieces):
        row_group, code_group = pieces
        lut_rows = lookup_rows(row_group, codebook)
        one_hot = code_one_hot(code_group)
        scores = jnp.einsum("grk,gkl->grl", lut_rows, one_hot, preferred_element_type=jnp.float32)
        top_score = jnp.max(scores, axis=2)
        exp_total = jnp.sum(jnp.exp(scores - top_score[:, :, None]), axis=2)
        return (scores, top_score, exp_total)

    scores, top_score, exp_total = lax.map(
        score_piece,
        (
            got_rows.reshape(groups, group_width, slot_rows, D),
            passage_codes.reshape(groups, group_width, SUBSPACES, PASSAGES),
        ),
    )
    return (
        scores.reshape(lists_dev, slot_rows, PASSAGES),
        top_score.reshape(lists_dev, slot_rows),
        exp_total.reshape(lists_dev, slot_rows),
    )


def second_pass(
    got_rows, got_notes, passage_codes, codebook, scores, query_top, query_total, group_width
):
    lists_dev, slot_rows = (got_rows.shape[0], got_rows.shape[1])
    groups = lists_dev // group_width
    weights = rank_weights()
    places = jnp.arange(PASSAGES, dtype=jnp.int32)
    centroids = codebook.reshape(CENTROIDS, SUBSPACES, SUBDIM)
    highest = lax.Precision.HIGHEST

    def grad_piece(pieces):
        row_group, note_group, code_group, score_group, top_group, total_group = pieces
        one_hot = code_one_hot(code_group)
        target_spot = note_group[:, :, 1:]
        teacher = jnp.sum(
            jnp.where(target_spot[:, :, :, None] == places, weights[:, None], 0.0), axis=2
        )
        student = jnp.exp(score_group - top_group[:, :, None]) / total_group[:, :, None]
        is_valid = note_group[:, :, 0] >= 0
        grad_scores = jnp.where(is_valid[:, :, None], student - teacher, 0.0).astype(jnp.bfloat16)
        histogram = jnp.einsum(
            "grl,gkl->grk", grad_scores, one_hot, preferred_element_type=jnp.float32
        )
        histogram = histogram.reshape(group_width, slot_rows, SUBSPACES, CENTROIDS)
        partial_value = jnp.einsum("grmk,kme->grme", histogram, centroids, precision=highest)
        split_rows = row_group.astype(jnp.float32).reshape(
            group_width, slot_rows, SUBSPACES, SUBDIM
        )
        book_part = jnp.einsum("grmk,grme->kme", histogram, split_rows, precision=highest)
        return (partial_value.reshape(group_width, slot_rows, D), book_part)

    partial_value, book_part = lax.map(
        grad_piece,
        (
            got_rows.reshape(groups, group_width, slot_rows, D),
            got_notes.reshape(groups, group_width, slot_rows, TARGETS + 1),
            passage_codes.reshape(groups, group_width, SUBSPACES, PASSAGES),
            scores.reshape(groups, group_width, slot_rows, PASSAGES),
            query_top.reshape(groups, group_width, slot_rows),
            query_total.reshape(groups, group_width, slot_rows),
        ),
    )
    return (
        partial_value.reshape(lists_dev, slot_rows, D),
        jnp.sum(book_part, axis=0).reshape(CENTROIDS, D),
    )


def shards(queries, probes, targets, passage_codes, codebook):
    corpus_size = lax.axis_size("corpus")
    query_rows = queries.shape[0]
    lists_dev = passage_codes.shape[0]
    list_total = lists_dev * corpus_size
    capacity = min(query_rows, max(2, 2 * PROBES * query_rows // list_total))
    slot_rows = corpus_size * capacity
    slot_count = lists_dev * slot_rows
    group_width = group_size(lists_dev, slot_rows)
    flat_probes = probes.reshape(-1)
    local_list = flat_probes % lists_dev
    owner_ids = flat_probes // lists_dev
    slot_rank = rank_slots(flat_probes, list_total, jnp.ones(flat_probes.shape, jnp.bool_))
    note_rows = note_block(probes, targets)
    placed = (local_list * corpus_size + owner_ids) * capacity + slot_rank
    sending = (
        jnp.zeros((slot_count, D), jnp.bfloat16).at[placed].set(jnp.repeat(queries, PROBES, axis=0))
    )
    note_buffer = jnp.full((slot_count, TARGETS + 1), -1, jnp.int32).at[placed].set(note_rows)
    got_rows, got_notes = (
        lax.all_to_all(
            sending.reshape(lists_dev, corpus_size, capacity, D),
            "corpus",
            split_axis=1,
            concat_axis=1,
            tiled=True,
        ),
        lax.all_to_all(
            note_buffer.reshape(lists_dev, corpus_size, capacity, TARGETS + 1),
            "corpus",
            split_axis=1,
            concat_axis=1,
            tiled=True,
        ),
    )
    got_rows = got_rows.reshape(lists_dev, slot_rows, D)
    got_notes = got_notes.reshape(lists_dev, slot_rows, TARGETS + 1)
    is_valid = got_notes[:, :, 0] >= 0
    scores, top_score, exp_total = first_pass(got_rows, passage_codes, codebook, group_width)
    top_score = jnp.where(is_valid, top_score, NEGATIVE)
    exp_total = jnp.where(is_valid, exp_total, 0.0)
    back_top, back_total = (
        lax.all_to_all(
            top_score.reshape(lists_dev, corpus_size, capacity),
            "corpus",
            split_axis=1,
            concat_axis=1,
            tiled=True,
        ),
        lax.all_to_all(
            exp_total.reshape(lists_dev, corpus_size, capacity),
            "corpus",
            split_axis=1,
            concat_axis=1,
            tiled=True,
        ),
    )
    entry_top = back_top.reshape(-1)[placed].reshape(query_rows, PROBES)
    entry_total = back_total.reshape(-1)[placed].reshape(query_rows, PROBES)
    own_top = jnp.max(entry_top, axis=1)
    own_total = jnp.sum(entry_total * jnp.exp(entry_top - own_top[:, None]), axis=1)
    slot_top = jnp.zeros((slot_count,), jnp.float32).at[placed].set(jnp.repeat(own_top, PROBES))
    slot_total = jnp.ones((slot_count,), jnp.float32).at[placed].set(jnp.repeat(own_total, PROBES))
    query_top, query_total = (
        lax.all_to_all(
            slot_top.reshape(lists_dev, corpus_size, capacity),
            "corpus",
            split_axis=1,
            concat_axis=1,
            tiled=True,
        ),
        lax.all_to_all(
            slot_total.reshape(lists_dev, corpus_size, capacity),
            "corpus",
            split_axis=1,
            concat_axis=1,
            tiled=True,
        ),
    )
    query_top = query_top.reshape(lists_dev, slot_rows)
    query_total = query_total.reshape(lists_dev, slot_rows)
    query_top = jnp.where(is_valid, query_top, 0.0)
    query_total = jnp.where(is_valid, query_total, 1.0)
    partial_value, book_part = second_pass(
        got_rows, got_notes, passage_codes, codebook, scores, query_top, query_total, group_width
    )
    returned = lax.all_to_all(
        partial_value.reshape(lists_dev, corpus_size, capacity, D),
        "corpus",
        split_axis=1,
        concat_axis=1,
        tiled=True,
    )
    per_probe = returned.reshape(slot_count, D)[placed].reshape(query_rows, PROBES, D)
    grad_queries = jnp.sum(per_probe, axis=1)
    book_sum = lax.psum(book_part, ("corpus", "query"))
    normed = book_sum * lax.rsqrt(jnp.mean(book_sum * book_sum) + EPSILON)
    return (grad_queries.astype(jnp.bfloat16), normed)


def solution(mesh):
    placed = (
        P(("corpus", "query"), None),
        P(("corpus", "query"), None),
        P(("corpus", "query"), None),
        P("corpus", None, None),
        P(),
    )
    return jax.shard_map(
        shards,
        mesh=mesh,
        in_specs=placed,
        out_specs=(P(("corpus", "query"), None), P()),
        check_vma=False,
    )
```

profile of v0, /device:TPU:0, one launch (start us, length us, event | category | flops | bytes accessed | tf_op | source)
XLA Modules:
  0.0 720.0 jit_solution(10076613516006259943)
XLA Ops:
  9.2 7.3 %all-to-all-start = ((s32[8,1,2304]{2,1,0:T(1,128)}), s32[8,1,2304]{2,1,0:T(1,128)S(1)}, u32[]{:S(2)}, u32[]{:S(2)}) async-start(s32[8,1,2304]{2,1,0:T(1,128)} %reshape.395), calls=%async_computation | async-start | bytes 147456 | tf_op jit(solution)/shard_map/all_to_all | solution.py:175
  18.3 6.8 scatter_custom_fusion.1
  27.6 6.3 all-to-all-start.1
  41.2 62.9 %all-to-all-done.1 = bf16[32,8,8,768]{3,2,0,1:T(8,128)(2,1)S(1)} async-done(((bf16[32,8,8,768]{3,2,0,1:T(8,128)(2,1)}), bf16[32,8,8,768]{3,2,0,1:T(8,128)(2,1)S(1)}, u32[]{:S(2)}, u32[]{:S(2)}) %all-to-all-start.1) | async-done | bytes 3145760 | tf_op jit(solution)/shard_map/all_to_all | solution.py:168
  106.1 6.6 copy.131
  113.9 129.6 %while.27 = (s32[]{:T(128)}, f32[4,8,64,1024]{3,2,1,0:T(8,128)}, f32[4,8,64]{2,1,0:T(8,128)}, f32[4,8,64]{2,1,0:T(8,128)}, bf16[4,8,64,768]{2,3,1,0:T(8,128)(2,1...) while((s32[]{:T(128)}, f32[4,8,64,1024]{3,2,1,0:T(8,128)}, ...), condition=%wide.region_8.9_spmd, body=%wide.region_5.8_spmd.sunk | while | flops 1701051392 | bytes 57241216 | solution.py:86
  124.0 9.4 %bitcast_compare_fusion.4 = pred[8,1536,1024]{2,1,0:T(32,128)(4,1)} fusion(s32[1536]{0:T(1024)S(1)} %eq.177, s32[8,96,1024]{2,1,0:T(8,128)S(1)} %dynamic-slice_bitcast_fusion.14), kind=kLoop, calls=%fused_computation.9.clone.1 | loop fusion | flops 12582912 | bytes 15734784 | tf_op jit(solution)/shard_map/while/body/eval_jaxpr/eq | solution.py:56
  133.3 11.7 %bitcast_dynamic-update-slice_fusion.5 = (f32[4,8,64,1024]{3,2,1,0:T(8,128)}, f32[8,64,1024]{2,1,0:T(8,128)S(1)}) fusion(f32[4,8,64,1024]{3,2,1,0:T(8,128)} %get-tuple-element.387, s32[]{:T(128)} %get-tuple-element.386, bf16[8,64,1536]{1,2,0:T(8,128)(2,1)S(1)} %bitcast.182, pred[8,1536,1024]{2,1,0:T(32,128)(4,1)} %bitcast_compare_fusion.4), kind=kOutput, calls=%fused_computation.12.clone.1 | convolution fusion | flops 1610612736 | bytes 18350592 | tf_op jit(solution)/shard_map/while/body/eval_jaxpr/grk,gkl->grl/dot_general | solution.py:81
  156.4 9.4 %bitcast_compare_fusion.4 = pred[8,1536,1024]{2,1,0:T(32,128)(4,1)} fusion(s32[1536]{0:T(1024)S(1)} %eq.177, s32[8,96,1024]{2,1,0:T(8,128)S(1)} %dynamic-slice_bitcast_fusion.14), kind=kLoop, calls=%fused_computation.9.clone.1 | loop fusion | flops 12582912 | bytes 15734784 | tf_op jit(solution)/shard_map/while/body/eval_jaxpr/eq | solution.py:56
  165.8 11.7 %bitcast_dynamic-update-slice_fusion.5 = (f32[4,8,64,1024]{3,2,1,0:T(8,128)}, f32[8,64,1024]{2,1,0:T(8,128)S(1)}) fusion(f32[4,8,64,1024]{3,2,1,0:T(8,128)} %get-tuple-element.387, s32[]{:T(128)} %get-tuple-element.386, bf16[8,64,1536]{1,2,0:T(8,128)(2,1)S(1)} %bitcast.182, pred[8,1536,1024]{2,1,0:T(32,128)(4,1)} %bitcast_compare_fusion.4), kind=kOutput, calls=%fused_computation.12.clone.1 | convolution fusion | flops 1610612736 | bytes 18350592 | tf_op jit(solution)/shard_map/while/body/eval_jaxpr/grk,gkl->grl/dot_general | solution.py:81
  188.8 9.4 %bitcast_compare_fusion.4 = pred[8,1536,1024]{2,1,0:T(32,128)(4,1)} fusion(s32[1536]{0:T(1024)S(1)} %eq.177, s32[8,96,1024]{2,1,0:T(8,128)S(1)} %dynamic-slice_bitcast_fusion.14), kind=kLoop, calls=%fused_computation.9.clone.1 | loop fusion | flops 12582912 | bytes 15734784 | tf_op jit(solution)/shard_map/while/body/eval_jaxpr/eq | solution.py:56
  198.2 11.7 %bitcast_dynamic-update-slice_fusion.5 = (f32[4,8,64,1024]{3,2,1,0:T(8,128)}, f32[8,64,1024]{2,1,0:T(8,128)S(1)}) fusion(f32[4,8,64,1024]{3,2,1,0:T(8,128)} %get-tuple-element.387, s32[]{:T(128)} %get-tuple-element.386, bf16[8,64,1536]{1,2,0:T(8,128)(2,1)S(1)} %bitcast.182, pred[8,1536,1024]{2,1,0:T(32,128)(4,1)} %bitcast_compare_fusion.4), kind=kOutput, calls=%fused_computation.12.clone.1 | convolution fusion | flops 1610612736 | bytes 18350592 | tf_op jit(solution)/shard_map/while/body/eval_jaxpr/grk,gkl->grl/dot_general | solution.py:81
  221.2 9.4 %bitcast_compare_fusion.4 = pred[8,1536,1024]{2,1,0:T(32,128)(4,1)} fusion(s32[1536]{0:T(1024)S(1)} %eq.177, s32[8,96,1024]{2,1,0:T(8,128)S(1)} %dynamic-slice_bitcast_fusion.14), kind=kLoop, calls=%fused_computation.9.clone.1 | loop fusion | flops 12582912 | bytes 15734784 | tf_op jit(solution)/shard_map/while/body/eval_jaxpr/eq | solution.py:56
  230.6 11.7 %bitcast_dynamic-update-slice_fusion.5 = (f32[4,8,64,1024]{3,2,1,0:T(8,128)}, f32[8,64,1024]{2,1,0:T(8,128)S(1)}) fusion(f32[4,8,64,1024]{3,2,1,0:T(8,128)} %get-tuple-element.387, s32[]{:T(128)} %get-tuple-element.386, bf16[8,64,1536]{1,2,0:T(8,128)(2,1)S(1)} %bitcast.182, pred[8,1536,1024]{2,1,0:T(32,128)(4,1)} %bitcast_compare_fusion.4), kind=kOutput, calls=%fused_computation.12.clone.1 | convolution fusion | flops 1610612736 | bytes 18350592 | tf_op jit(solution)/shard_map/while/body/eval_jaxpr/grk,gkl->grl/dot_general | solution.py:81
  251.2 5.8 all-to-all-done.2
  261.8 6.2 gather_fusion
  269.3 6.2 gather_fusion.1
  276.0 4.3 scatter_custom_fusion.3
  281.2 5.9 all-to-all-start.5
  287.4 4.3 scatter_custom_fusion.2
  293.6 4.9 all-to-all-start.3
  300.4 4.7 all-to-all-done.3
  306.0 221.0 %while.28 = (s32[]{:T(128)}, f32[4,8,64,768]{3,2,1,0:T(8,128)}, f32[4,16,96,8]{1,3,2,0:T(8,128)}, s32[4,8,64,9]{2,1,0,3:T(8,128)S(1)}, f32[4,8,64,1024]{3,2,1,0:...) while((s32[]{:T(128)}, f32[4,8,64,768]{3,2,1,0:T(8,128)}, ...), condition=%wide.region_15.16_spmd.clone, body=%wide.region_13.15_spmd.clone.sunk | while | flops 1788871168 | bytes 67385192 | solution.py:131
  315.8 7.1 select_reduce_fusion.2
  327.1 9.3 %bitcast_compare_fusion.5 = pred[8,1536,1024]{2,1,0:T(32,128)(4,1)} fusion(s32[1536]{0:T(1024)S(1)} %eq.184, s32[8,96,1024]{2,1,0:T(8,128)S(1)} %dynamic-slice_bitcast_fusion.15), kind=kLoop, calls=%fused_computation.19.clone.1 | loop fusion | flops 12582912 | bytes 15734784 | tf_op jit(solution)/shard_map/while/body/eval_jaxpr/eq | solution.py:56
  336.5 12.8 %fusion.86 = f32[8,64,1536]{1,2,0:T(8,128)} fusion(pred[8,1536,1024]{2,1,0:T(32,128)(4,1)} %bitcast_compare_fusion.5, f32[8,64,1024]{2,1,0:T(8,128)} %select_reduce_fusion.2, f32[4,8,64,1024]{3,2,1,0:T(8,128)} %get-tuple-element.430, s32[]{:T(128)} %get-tuple-element.415, f32[8,64]{1,0:T(8,128)S(1)} %get-tuple-element.375, ...), kind=kOutput, calls=%fused_computation.38.clone.1 | convolution fusion | flops 1613234176 | bytes 19928576 | tf_op jit(solution)/shard_map/while/body/eval_jaxpr/grl,gkl->grk/dot_general | solution.py:120
  349.3 5.5 fusion.87
  359.7 8.3 %fusion.88 = f32[4,16,96,8]{1,3,2,0:T(8,128)} fusion(f32[4,16,96,8]{1,3,2,0:T(8,128)} %get-tuple-element.417, s32[]{:T(128)} %get-tuple-element.415, f32[8,64,96,16]{1,3,2,0:T(8,128)} %bitcast.181, bf16[4,8,64,768]{2,3,1,0:T(8,128)(2,1)} %get-tuple-element.435), kind=kOutput, calls=%fused_computation.37.clone.1 | convolution fusion | flops 75497472 | bytes 8258560 | tf_op jit(solution)/shard_map/while/body/eval_jaxpr/grmk,grme->kme/dot_general | solution.py:128
  368.7 7.1 select_reduce_fusion.2
  380.1 9.3 %bitcast_compare_fusion.5 = pred[8,1536,1024]{2,1,0:T(32,128)(4,1)} fusion(s32[1536]{0:T(1024)S(1)} %eq.184, s32[8,96,1024]{2,1,0:T(8,128)S(1)} %dynamic-slice_bitcast_fusion.15), kind=kLoop, calls=%fused_computation.19.clone.1 | loop fusion | flops 12582912 | bytes 15734784 | tf_op jit(solution)/shard_map/while/body/eval_jaxpr/eq | solution.py:56
  389.4 12.8 %fusion.86 = f32[8,64,1536]{1,2,0:T(8,128)} fusion(pred[8,1536,1024]{2,1,0:T(32,128)(4,1)} %bitcast_compare_fusion.5, f32[8,64,1024]{2,1,0:T(8,128)} %select_reduce_fusion.2, f32[4,8,64,1024]{3,2,1,0:T(8,128)} %get-tuple-element.430, s32[]{:T(128)} %get-tuple-element.415, f32[8,64]{1,0:T(8,128)S(1)} %get-tuple-element.375, ...), kind=kOutput, calls=%fused_computation.38.clone.1 | convolution fusion | flops 1613234176 | bytes 19928576 | tf_op jit(solution)/shard_map/while/body/eval_jaxpr/grl,gkl->grk/dot_general | solution.py:120
  402.2 5.5 fusion.87
  412.6 8.2 %fusion.88 = f32[4,16,96,8]{1,3,2,0:T(8,128)} fusion(f32[4,16,96,8]{1,3,2,0:T(8,128)} %get-tuple-element.417, s32[]{:T(128)} %get-tuple-element.415, f32[8,64,96,16]{1,3,2,0:T(8,128)} %bitcast.181, bf16[4,8,64,768]{2,3,1,0:T(8,128)(2,1)} %get-tuple-element.435), kind=kOutput, calls=%fused_computation.37.clone.1 | convolution fusion | flops 75497472 | bytes 8258560 | tf_op jit(solution)/shard_map/while/body/eval_jaxpr/grmk,grme->kme/dot_general | solution.py:128
  421.7 7.1 select_reduce_fusion.2
  433.0 9.3 %bitcast_compare_fusion.5 = pred[8,1536,1024]{2,1,0:T(32,128)(4,1)} fusion(s32[1536]{0:T(1024)S(1)} %eq.184, s32[8,96,1024]{2,1,0:T(8,128)S(1)} %dynamic-slice_bitcast_fusion.15), kind=kLoop, calls=%fused_computation.19.clone.1 | loop fusion | flops 12582912 | bytes 15734784 | tf_op jit(solution)/shard_map/while/body/eval_jaxpr/eq | solution.py:56
  442.3 12.8 %fusion.86 = f32[8,64,1536]{1,2,0:T(8,128)} fusion(pred[8,1536,1024]{2,1,0:T(32,128)(4,1)} %bitcast_compare_fusion.5, f32[8,64,1024]{2,1,0:T(8,128)} %select_reduce_fusion.2, f32[4,8,64,1024]{3,2,1,0:T(8,128)} %get-tuple-element.430, s32[]{:T(128)} %get-tuple-element.415, f32[8,64]{1,0:T(8,128)S(1)} %get-tuple-element.375, ...), kind=kOutput, calls=%fused_computation.38.clone.1 | convolution fusion | flops 1613234176 | bytes 19928576 | tf_op jit(solution)/shard_map/while/body/eval_jaxpr/grl,gkl->grk/dot_general | solution.py:120
  455.2 5.5 fusion.87
  465.6 8.2 %fusion.88 = f32[4,16,96,8]{1,3,2,0:T(8,128)} fusion(f32[4,16,96,8]{1,3,2,0:T(8,128)} %get-tuple-element.417, s32[]{:T(128)} %get-tuple-element.415, f32[8,64,96,16]{1,3,2,0:T(8,128)} %bitcast.181, bf16[4,8,64,768]{2,3,1,0:T(8,128)(2,1)} %get-tuple-element.435), kind=kOutput, calls=%fused_computation.37.clone.1 | convolution fusion | flops 75497472 | bytes 8258560 | tf_op jit(solution)/shard_map/while/body/eval_jaxpr/grmk,grme->kme/dot_general | solution.py:128
  474.7 7.1 select_reduce_fusion.2
  486.0 9.3 %bitcast_compare_fusion.5 = pred[8,1536,1024]{2,1,0:T(32,128)(4,1)} fusion(s32[1536]{0:T(1024)S(1)} %eq.184, s32[8,96,1024]{2,1,0:T(8,128)S(1)} %dynamic-slice_bitcast_fusion.15), kind=kLoop, calls=%fused_computation.19.clone.1 | loop fusion | flops 12582912 | bytes 15734784 | tf_op jit(solution)/shard_map/while/body/eval_jaxpr/eq | solution.py:56
  495.4 12.8 %fusion.86 = f32[8,64,1536]{1,2,0:T(8,128)} fusion(pred[8,1536,1024]{2,1,0:T(32,128)(4,1)} %bitcast_compare_fusion.5, f32[8,64,1024]{2,1,0:T(8,128)} %select_reduce_fusion.2, f32[4,8,64,1024]{3,2,1,0:T(8,128)} %get-tuple-element.430, s32[]{:T(128)} %get-tuple-element.415, f32[8,64]{1,0:T(8,128)S(1)} %get-tuple-element.375, ...), kind=kOutput, calls=%fused_computation.38.clone.1 | convolution fusion | flops 1613234176 | bytes 19928576 | tf_op jit(solution)/shard_map/while/body/eval_jaxpr/grl,gkl->grk/dot_general | solution.py:120
  508.2 5.5 fusion.87
  518.6 8.2 %fusion.88 = f32[4,16,96,8]{1,3,2,0:T(8,128)} fusion(f32[4,16,96,8]{1,3,2,0:T(8,128)} %get-tuple-element.417, s32[]{:T(128)} %get-tuple-element.415, f32[8,64,96,16]{1,3,2,0:T(8,128)} %bitcast.181, bf16[4,8,64,768]{2,3,1,0:T(8,128)(2,1)} %get-tuple-element.435), kind=kOutput, calls=%fused_computation.37.clone.1 | convolution fusion | flops 75497472 | bytes 8258560 | tf_op jit(solution)/shard_map/while/body/eval_jaxpr/grmk,grme->kme/dot_general | solution.py:128
  527.0 6.0 copy.147
  533.1 4.9 all-to-all-start.6
  538.1 158.5 %psum.7 = f32[16,768]{0,1:T(8,128)S(1)} all-reduce(f32[16,768]{0,1:T(8,128)S(1)} %bitcast.194), channel_id=1, replica_groups=mesh['corpus'=8,'query'=4] {'corpus','query'}, use_global_device_ids=true, to_apply=%region_18.19 | all-reduce | flops 12288 | bytes 98304 | tf_op jit(solution)/shard_map/psum | solution.py:243
  698.8 6.3 copy.148
  705.1 8.6 %gather_fusion.2 = f32[1024,768]{1,0:T(8,128)} fusion(f32[2048,768]{1,0:T(8,128)} %bitcast.184, s32[1024]{0:T(1024)S(1)} %copy-done.12), kind=kCustom, calls=%fused_computation.2 | custom fusion | bytes 6295552 | tf_op jit(solution)/shard_map/gather | solution.py:241
  (247 shorter events, 135.3 us)
Async XLA Ops:
  1.9 1.1 copy-start.13
  3.8 12.7 %copy-start.5 = (bf16[256,768]{1,0:T(8,128)(2,1)S(1)}, bf16[256,768]{1,0:T(8,128)(2,1)}, u32[]{:S(2)}) copy-start(bf16[256,768]{1,0:T(8,128)(2,1)} %param.9) | copy-start | bytes 1179652
  9.2 17.8 %all-to-all-start = ((s32[8,1,2304]{2,1,0:T(1,128)}), s32[8,1,2304]{2,1,0:T(1,128)S(1)}, u32[]{:S(2)}, u32[]{:S(2)}) async-start(s32[8,1,2304]{2,1,0:T(1,128)} %reshape.395), calls=%async_computation | async-start | bytes 147456 | tf_op jit(solution)/shard_map/all_to_all | solution.py:175
  27.0 0.6 copy-start.6
  27.6 76.4 %all-to-all-start.1 = ((bf16[32,8,8,768]{3,2,0,1:T(8,128)(2,1)}), bf16[32,8,8,768]{3,2,0,1:T(8,128)(2,1)S(1)}, u32[]{:S(2)}, u32[]{:S(2)}) async-start(bf16[32,8,8,768]{3,2,0,1:T(8,128)(2,1)} %copy.129), calls=%async_computation.1 | async-start | bytes 6291456 | tf_op jit(solution)/shard_map/all_to_all | solution.py:168
  124.0 9.4 %copy-start = (bf16[8,64,96,16]{1,3,2,0:T(8,128)(2,1)S(1)}, bf16[8,64,96,16]{1,3,2,0:T(8,128)(2,1)}, u32[]{:S(2)}) copy-start(bf16[8,64,96,16]{1,3,2,0:T(8,128)(2,1)} %copy.181) | copy-start | bytes 4718596 | tf_op jit(solution)/shard_map/while
  156.4 9.4 %copy-start = (bf16[8,64,96,16]{1,3,2,0:T(8,128)(2,1)S(1)}, bf16[8,64,96,16]{1,3,2,0:T(8,128)(2,1)}, u32[]{:S(2)}) copy-start(bf16[8,64,96,16]{1,3,2,0:T(8,128)(2,1)} %copy.181) | copy-start | bytes 4718596 | tf_op jit(solution)/shard_map/while
  188.8 9.4 %copy-start = (bf16[8,64,96,16]{1,3,2,0:T(8,128)(2,1)S(1)}, bf16[8,64,96,16]{1,3,2,0:T(8,128)(2,1)}, u32[]{:S(2)}) copy-start(bf16[8,64,96,16]{1,3,2,0:T(8,128)(2,1)} %copy.181) | copy-start | bytes 4718596 | tf_op jit(solution)/shard_map/while
  221.2 9.4 %copy-start = (bf16[8,64,96,16]{1,3,2,0:T(8,128)(2,1)S(1)}, bf16[8,64,96,16]{1,3,2,0:T(8,128)(2,1)}, u32[]{:S(2)}) copy-start(bf16[8,64,96,16]{1,3,2,0:T(8,128)(2,1)} %copy.181) | copy-start | bytes 4718596 | tf_op jit(solution)/shard_map/while
  246.8 10.2 %all-to-all-start.2 = ((f32[8,1,256]{2,1,0:T(1,128)}), f32[8,1,256]{2,1,0:T(1,128)S(1)}, u32[]{:S(2)}, u32[]{:S(2)}) async-start(f32[8,1,256]{2,1,0:T(1,128)} %reshape.397), calls=%async_computation.2 | async-start | bytes 16384 | tf_op jit(solution)/shard_map/all_to_all | solution.py:190
  257.0 11.3 %all-to-all-start.4 = ((f32[8,1,256]{2,1,0:T(1,128)}), f32[8,1,256]{2,1,0:T(1,128)S(1)}, u32[]{:S(2)}, u32[]{:S(2)}) async-start(f32[8,1,256]{2,1,0:T(1,128)} %reshape.401), calls=%async_computation.4 | async-start | bytes 16384 | tf_op jit(solution)/shard_map/all_to_all | solution.py:197
  260.3 15.1 %copy-start.11 = (s32[1024]{0:T(1024)}, s32[1024]{0:T(1024)S(1)}, u32[]{:S(2)}) copy-start(s32[1024]{0:T(1024)S(1)} %broadcast_clamp_fusion) | copy-start | bytes 12292
  268.2 30.3 %copy-start.1 = (s32[8,9,8,32]{3,2,1,0:T(8,128)S(1)}, s32[8,9,8,32]{3,2,1,0:T(8,128)}, u32[]{:S(2)}) copy-start(s32[8,9,8,32]{3,2,1,0:T(8,128)} %reshape.396) | copy-start | bytes 221188
  281.2 12.4 %all-to-all-start.5 = ((f32[8,1,256]{2,1,0:T(1,128)}), f32[8,1,256]{2,1,0:T(1,128)S(1)}, u32[]{:S(2)}, u32[]{:S(2)}) async-start(f32[8,1,256]{2,1,0:T(1,128)} %reshape.403), calls=%async_computation.5 | async-start | bytes 16384 | tf_op jit(solution)/shard_map/all_to_all | solution.py:219
  293.6 11.4 %all-to-all-start.3 = ((f32[8,1,256]{2,1,0:T(1,128)}), f32[8,1,256]{2,1,0:T(1,128)S(1)}, u32[]{:S(2)}, u32[]{:S(2)}) async-start(f32[8,1,256]{2,1,0:T(1,128)} %reshape.399), calls=%async_computation.3 | async-start | bytes 16384 | tf_op jit(solution)/shard_map/all_to_all | solution.py:212
  315.0 0.6 copy-start.7
  315.0 0.6 copy-start.9
  315.0 8.5 %copy-start.3 = (s32[4,8,64,9]{2,1,0,3:T(8,128)}, s32[4,8,64,9]{2,1,0,3:T(8,128)S(1)}, u32[]{:S(2)}) copy-start(s32[4,8,64,9]{2,1,0,3:T(8,128)S(1)} %get-tuple-element.429) | copy-start | bytes 221188 | tf_op jit(solution)/shard_map/while
  359.7 8.3 %copy-start.4 = (s32[4,8,64,9]{2,1,0,3:T(8,128)S(1)}, s32[4,8,64,9]{2,1,0,3:T(8,128)}, u32[]{:S(2)}) copy-start(s32[4,8,64,9]{2,1,0,3:T(8,128)} %copy-done.3) | copy-start | bytes 221188 | tf_op jit(solution)/shard_map/while
  359.7 8.3 %copy-start.8 = (f32[4,8,64]{2,1,0:T(8,128)S(1)}, f32[4,8,64]{2,1,0:T(8,128)}, u32[]{:S(2)}) copy-start(f32[4,8,64]{2,1,0:T(8,128)} %copy-done.7) | copy-start | bytes 24580 | tf_op jit(solution)/shard_map/while
  359.7 8.3 %copy-start.10 = (f32[4,8,64]{2,1,0:T(8,128)S(1)}, f32[4,8,64]{2,1,0:T(8,128)}, u32[]{:S(2)}) copy-start(f32[4,8,64]{2,1,0:T(8,128)} %copy-done.9) | copy-start | bytes 24580 | tf_op jit(solution)/shard_map/while
  368.0 0.6 copy-start.7
  368.0 0.6 copy-start.9
  368.0 8.5 %copy-start.3 = (s32[4,8,64,9]{2,1,0,3:T(8,128)}, s32[4,8,64,9]{2,1,0,3:T(8,128)S(1)}, u32[]{:S(2)}) copy-start(s32[4,8,64,9]{2,1,0,3:T(8,128)S(1)} %get-tuple-element.429) | copy-start | bytes 221188 | tf_op jit(solution)/shard_map/while
  412.6 8.2 %copy-start.4 = (s32[4,8,64,9]{2,1,0,3:T(8,128)S(1)}, s32[4,8,64,9]{2,1,0,3:T(8,128)}, u32[]{:S(2)}) copy-start(s32[4,8,64,9]{2,1,0,3:T(8,128)} %copy-done.3) | copy-start | bytes 221188 | tf_op jit(solution)/shard_map/while
  412.6 8.2 %copy-start.8 = (f32[4,8,64]{2,1,0:T(8,128)S(1)}, f32[4,8,64]{2,1,0:T(8,128)}, u32[]{:S(2)}) copy-start(f32[4,8,64]{2,1,0:T(8,128)} %copy-done.7) | copy-start | bytes 24580 | tf_op jit(solution)/shard_map/while
  412.6 8.2 %copy-start.10 = (f32[4,8,64]{2,1,0:T(8,128)S(1)}, f32[4,8,64]{2,1,0:T(8,128)}, u32[]{:S(2)}) copy-start(f32[4,8,64]{2,1,0:T(8,128)} %copy-done.9) | copy-start | bytes 24580 | tf_op jit(solution)/shard_map/while
  420.9 0.6 copy-start.7
  420.9 0.6 copy-start.9
  420.9 8.5 %copy-start.3 = (s32[4,8,64,9]{2,1,0,3:T(8,128)}, s32[4,8,64,9]{2,1,0,3:T(8,128)S(1)}, u32[]{:S(2)}) copy-start(s32[4,8,64,9]{2,1,0,3:T(8,128)S(1)} %get-tuple-element.429) | copy-start | bytes 221188 | tf_op jit(solution)/shard_map/while
  465.6 8.3 %copy-start.4 = (s32[4,8,64,9]{2,1,0,3:T(8,128)S(1)}, s32[4,8,64,9]{2,1,0,3:T(8,128)}, u32[]{:S(2)}) copy-start(s32[4,8,64,9]{2,1,0,3:T(8,128)} %copy-done.3) | copy-start | bytes 221188 | tf_op jit(solution)/shard_map/while
  465.6 8.3 %copy-start.8 = (f32[4,8,64]{2,1,0:T(8,128)S(1)}, f32[4,8,64]{2,1,0:T(8,128)}, u32[]{:S(2)}) copy-start(f32[4,8,64]{2,1,0:T(8,128)} %copy-done.7) | copy-start | bytes 24580 | tf_op jit(solution)/shard_map/while
  465.6 8.3 %copy-start.10 = (f32[4,8,64]{2,1,0:T(8,128)S(1)}, f32[4,8,64]{2,1,0:T(8,128)}, u32[]{:S(2)}) copy-start(f32[4,8,64]{2,1,0:T(8,128)} %copy-done.9) | copy-start | bytes 24580 | tf_op jit(solution)/shard_map/while
  473.9 0.6 copy-start.7
  473.9 0.6 copy-start.9
  473.9 8.5 %copy-start.3 = (s32[4,8,64,9]{2,1,0,3:T(8,128)}, s32[4,8,64,9]{2,1,0,3:T(8,128)S(1)}, u32[]{:S(2)}) copy-start(s32[4,8,64,9]{2,1,0,3:T(8,128)S(1)} %get-tuple-element.429) | copy-start | bytes 221188 | tf_op jit(solution)/shard_map/while
  518.6 8.2 %copy-start.4 = (s32[4,8,64,9]{2,1,0,3:T(8,128)S(1)}, s32[4,8,64,9]{2,1,0,3:T(8,128)}, u32[]{:S(2)}) copy-start(s32[4,8,64,9]{2,1,0,3:T(8,128)} %copy-done.3) | copy-start | bytes 221188 | tf_op jit(solution)/shard_map/while
  518.6 8.2 %copy-start.8 = (f32[4,8,64]{2,1,0:T(8,128)S(1)}, f32[4,8,64]{2,1,0:T(8,128)}, u32[]{:S(2)}) copy-start(f32[4,8,64]{2,1,0:T(8,128)} %copy-done.7) | copy-start | bytes 24580 | tf_op jit(solution)/shard_map/while
  518.6 8.2 %copy-start.10 = (f32[4,8,64]{2,1,0:T(8,128)S(1)}, f32[4,8,64]{2,1,0:T(8,128)}, u32[]{:S(2)}) copy-start(f32[4,8,64]{2,1,0:T(8,128)} %copy-done.9) | copy-start | bytes 24580 | tf_op jit(solution)/shard_map/while
  533.1 4.9 copy-start.2
  533.1 165.7 %all-to-all-start.6 = ((f32[32,8,8,768]{3,2,0,1:T(8,128)}), f32[32,8,8,768]{3,2,0,1:T(8,128)}, u32[]{:S(2)}, u32[]{:S(2)}) async-start(f32[32,8,8,768]{3,2,0,1:T(8,128)} %copy.147), calls=%async_computation.6 | async-start | bytes 12582912 | tf_op jit(solution)/shard_map/all_to_all | solution.py:234
  698.8 6.3 copy-start.12
where the time goes:
time: 725 us; the launch traced here: 720 us
  matrix products  170 us (23%)
  blocking collectives  158 us (22%)
  local copies, waits for them, and re-layouts  147 us (20%)
  other arithmetic  123 us (17%)
  waiting for transfers between devices  74.5 us (10%)
  starting transfers between devices  36.2 us (5%)
  loops' own time  9.72 us (1%)
    psum x1, blocking collectives, shards(): book_sum = lax.psum(book_part, ('corpus', 'query'))  158 us
    eq x8, other arithmetic, code_one_hot(): marked = code_block[:, :, None, :] == levels[None, None, :, None]  74.8 us
    all_to_all x1, waiting for transfers between devices, shards(): lax.all_to_all(sending.reshape(lists_dev, corpus_size, capacity, D), 'cor...  62.9 us
    dot_general x4, matrix products, grad_piece(): jnp.einsum('grl,gkl->grk', grad_scores, one_hot, preferred_element_type=j...  51.3 us
    dot_general x4, matrix products, score_piece(): jnp.einsum('grk,gkl->grl', lut_rows, one_hot, preferred_element_type=jnp....  46.8 us
    dot_general x4, matrix products, grad_piece(): jnp.einsum('grmk,grme->kme', histogram, split_rows, precision=highest)  33 us
    eq x24, local copies, waits for them, and re-layouts, code_one_hot(): marked = code_block[:, :, None, :] == levels[None, None, :, None]  28.9 us
    reduce_sum x4, other arithmetic, grad_piece(): jnp.sum(jnp.where(target_spot[:, :, :, None] == places, weights[:, None],...  28.5 us
  transfers between devices with their start and end apart: 7, of which 4 were waited for; matrix products, arithmetic and copies ran while one was open for 5% of the time, Pallas kernels for 0%

commit v1 on v0

v1 whole, which is shorter than its diff:
```python
import functools

import jax
import jax.numpy as jnp
from jax import lax
from jax.experimental import pallas as pl
from jax.experimental.pallas import tpu as pltpu
from jax.sharding import PartitionSpec as P

D = 768
SUBSPACES = 96
CENTROIDS = 16
SUBDIM = 8
PASSAGES = 1024
PROBES = 4
TARGETS = 8
EPSILON = 1e-06

CHUNK = 128
CHUNKS = D // CHUNK
SPACES = CHUNK // SUBDIM
COLS = SPACES * CENTROIDS
NOTES = 128
WIDE = D + NOTES

NT = (((1,), (1,)), ((), ()))
TN = (((0,), (0,)), ((), ()))


def dot(a, b, dims=(((1,), (0,)), ((), ()))):
    return lax.dot_general(a, b, dims, preferred_element_type=jnp.float32)


def split(x, parts):
    out = []
    for _ in range(parts):
        top = x.astype(jnp.bfloat16)
        out.append(top)
        x = x - top.astype(jnp.float32)
    return out


def diagonal(shape):
    row = lax.broadcasted_iota(jnp.int32, shape, 1)
    col = lax.broadcasted_iota(jnp.int32, shape, 2)
    return row == col // SUBDIM


def fill_table(cb_ref, table):
    for c in range(CHUNKS):
        cb = cb_ref[:, c * CHUNK : (c + 1) * CHUNK]
        spread = jnp.broadcast_to(cb[:, None, :], (CENTROIDS, SPACES, CHUNK))
        spread = jnp.where(diagonal(spread.shape), spread, 0.0).reshape(COLS, CHUNK)
        for i, part in enumerate(split(spread, 3)):
            table[i, c] = part


def one_hot(codes_ref, c):
    codes = codes_ref[0, c * SPACES : (c + 1) * SPACES, :]
    return jnp.concatenate(
        [jnp.where(codes == k, 1.0, 0.0).astype(jnp.bfloat16) for k in range(CENTROIDS)], axis=0
    )


def score_kernel(off_ref, rows_ref, codes_ref, cb_ref, exp_ref, stat_ref, table):
    @pl.when(pl.program_id(0) == 0)
    def _():
        fill_table(cb_ref, table)

    scores = None
    for c in range(CHUNKS):
        row = rows_ref[0, :, c * CHUNK : (c + 1) * CHUNK]
        lut = dot(row, table[2, c], NT) + dot(row, table[1, c], NT) + dot(row, table[0, c], NT)
        term = dot(lut.astype(jnp.bfloat16), one_hot(codes_ref, c))
        scores = term if scores is None else scores + term
    top = jnp.max(scores, axis=1, keepdims=True)
    e = jnp.exp(scores - top)
    exp_ref[0] = e
    total = jnp.sum(e, axis=1, keepdims=True)
    lane = lax.broadcasted_iota(jnp.int32, (e.shape[0], 128), 1)
    stat_ref[0] = jnp.where(lane == 0, top, total).T[:8]


def grad_kernel(
    off_ref, rows_ref, codes_ref, cb_ref, exp_ref, factor_ref, part_ref, raw_ref, table, raw
):
    step = pl.program_id(0)

    @pl.when(step == 0)
    def _():
        fill_table(cb_ref, table)
        raw[...] = jnp.zeros_like(raw)

    slots = exp_ref.shape[1]
    factor = jnp.broadcast_to(factor_ref[0], (128, slots)).T[:, 0:1]
    notes = rows_ref[0, :, D:].astype(jnp.float32)
    place = lax.broadcasted_iota(jnp.int32, (slots, PASSAGES), 1)
    teacher = jnp.zeros((slots, PASSAGES), jnp.float32)
    for r in range(TARGETS):
        spot = (notes[:, r : r + 1] - 1.0) * 256.0 + notes[:, TARGETS + r : TARGETS + r + 1]
        weight = 2.0 * (TARGETS - r) / (TARGETS * (TARGETS + 1.0))
        teacher = jnp.where(place == spot.astype(jnp.int32), weight, teacher)
    grad = (exp_ref[0] * factor - teacher).astype(jnp.bfloat16)
    for c in range(CHUNKS):
        hist = dot(grad, one_hot(codes_ref, c), NT)
        hi, lo = split(hist, 2)
        part = dot(hi, table[0, c]) + dot(hi, table[1, c]) + dot(lo, table[0, c])
        part_ref[0, :, c * CHUNK : (c + 1) * CHUNK] = part.astype(jnp.bfloat16)
        row = rows_ref[0, :, c * CHUNK : (c + 1) * CHUNK]
        raw[c] += dot(hi, row, TN) + dot(lo, row, TN)

    @pl.when(step == pl.num_programs(0) - 1)
    def _():
        for c in range(CHUNKS):
            grid = raw[c].reshape(CENTROIDS, SPACES, CHUNK)
            kept = jnp.where(diagonal(grid.shape), grid, 0.0)
            raw_ref[:, c * CHUNK : (c + 1) * CHUNK] = jnp.sum(kept, axis=1)


def shards(queries, probes, targets, passage_codes, codebook):
    axes = ("corpus", "query")
    devices = lax.axis_size("corpus") * lax.axis_size("query")
    query_rows = queries.shape[0]
    list_total = passage_codes.shape[0] * lax.axis_size("corpus")
    lists = list_total // devices
    capacity = min(query_rows, max(2, 2 * PROBES * query_rows // list_total))
    slots = devices * capacity
    slot_count = lists * slots
    entries = PROBES * query_rows

    flat = probes.T.reshape(entries)
    ids = jnp.arange(entries, dtype=jnp.int32)
    earlier = (flat[:, None] == flat[None, :]) & (ids[None, :] < ids[:, None])
    rank = jnp.sum(earlier.astype(jnp.int32), axis=1)
    placed = ((flat % lists) * devices + flat // lists) * capacity + rank
    slot_ids = jnp.arange(slot_count, dtype=jnp.int32)
    hit = slot_ids[:, None] == placed[None, :]

    inside = targets[None] // PASSAGES == jnp.arange(PROBES, dtype=jnp.int32)[:, None, None]
    spot = targets[None] % PASSAGES
    notes = jnp.concatenate(
        [jnp.where(inside, spot // 256 + 1, 0), jnp.where(inside, spot % 256, 0)], axis=2
    ).reshape(entries, 2 * TARGETS)
    notes = jnp.pad(notes, ((0, 0), (0, NOTES - 2 * TARGETS))).astype(jnp.bfloat16)
    wide = jnp.concatenate([jnp.concatenate([queries] * PROBES, axis=0), notes], axis=1)
    sending = jnp.dot(
        hit.astype(jnp.bfloat16), wide, preferred_element_type=jnp.float32
    ).astype(jnp.bfloat16)

    def swap(x, axis=1):
        return lax.all_to_all(x, axes, split_axis=axis, concat_axis=axis, tiled=True)

    rows = swap(sending.reshape(lists, devices, capacity, WIDE)).reshape(lists, slots, WIDE)

    offset = (lax.axis_index("query") * lists).astype(jnp.int32).reshape(1)
    rows_spec = pl.BlockSpec((1, slots, WIDE), lambda i, off: (i, 0, 0))
    codes_spec = pl.BlockSpec((1, SUBSPACES, PASSAGES), lambda i, off: (off[0] + i, 0, 0))
    cb_spec = pl.BlockSpec((CENTROIDS, D), lambda i, off: (0, 0))
    exp_spec = pl.BlockSpec((1, slots, PASSAGES), lambda i, off: (i, 0, 0))
    table = pltpu.VMEM((3, CHUNKS, COLS, CHUNK), jnp.bfloat16)
    params = pltpu.CompilerParams(vmem_limit_bytes=40 * 2**20)

    exps, stats = pl.pallas_call(
        score_kernel,
        out_shape=(
            jax.ShapeDtypeStruct((lists, slots, PASSAGES), jnp.float32),
            jax.ShapeDtypeStruct((lists, 8, slots), jnp.float32),
        ),
        grid_spec=pltpu.PrefetchScalarGridSpec(
            num_scalar_prefetch=1,
            grid=(lists,),
            in_specs=[rows_spec, codes_spec, cb_spec],
            out_specs=(exp_spec, pl.BlockSpec((1, 8, slots), lambda i, off: (i, 0, 0))),
            scratch_shapes=[table],
        ),
        compiler_params=params,
        name="scores",
    )(offset, rows, passage_codes, codebook)

    back = swap(stats[:, :2].reshape(lists, 2, devices, capacity), 2)
    back_top = back[:, 0].reshape(slot_count)
    back_total = back[:, 1].reshape(slot_count)
    top = jnp.sum(jnp.where(hit, back_top[:, None], 0.0), axis=0).reshape(PROBES, query_rows)
    total = jnp.sum(jnp.where(hit, back_total[:, None], 0.0), axis=0).reshape(PROBES, query_rows)
    shrink = jnp.exp(top - jnp.max(top, axis=0))
    scale = (shrink / jnp.sum(total * shrink, axis=0)).reshape(entries)
    slot_scale = jnp.sum(jnp.where(hit, scale[None, :], 0.0), axis=1)
    factor = swap(slot_scale.reshape(lists, devices, capacity)).reshape(lists, 1, slots)

    part, raw = pl.pallas_call(
        grad_kernel,
        out_shape=(
            jax.ShapeDtypeStruct((lists, slots, D), jnp.bfloat16),
            jax.ShapeDtypeStruct((CENTROIDS, D), jnp.float32),
        ),
        grid_spec=pltpu.PrefetchScalarGridSpec(
            num_scalar_prefetch=1,
            grid=(lists,),
            in_specs=[
                rows_spec,
                codes_spec,
                cb_spec,
                exp_spec,
                pl.BlockSpec((1, 1, slots), lambda i, off: (i, 0, 0)),
            ],
            out_specs=(
                pl.BlockSpec((1, slots, D), lambda i, off: (i, 0, 0)),
                pl.BlockSpec((CENTROIDS, D), lambda i, off: (0, 0)),
            ),
            scratch_shapes=[table, pltpu.VMEM((CHUNKS, COLS, CHUNK), jnp.float32)],
        ),
        compiler_params=params,
        name="grads",
    )(offset, rows, passage_codes, codebook, exps, factor)

    raw = lax.psum(raw, axes)
    step = raw * lax.rsqrt(jnp.mean(raw * raw) + EPSILON)
    returned = swap(part.reshape(lists, devices, capacity, D)).reshape(slot_count, D)
    by_query = functools.reduce(
        jnp.logical_or,
        [
            slot_ids[None, :] == placed[p * query_rows : (p + 1) * query_rows, None]
            for p in range(PROBES)
        ],
    )
    grad = jnp.dot(by_query.astype(jnp.bfloat16), returned, preferred_element_type=jnp.float32)
    return (grad.astype(jnp.bfloat16), step)


def solution(mesh):
    placed = (
        P(("corpus", "query"), None),
        P(("corpus", "query"), None),
        P(("corpus", "query"), None),
        P("corpus", None, None),
        P(),
    )
    return jax.shard_map(
        shards,
        mesh=mesh,
        in_specs=placed,
        out_specs=(P(("corpus", "query"), None), P()),
        check_vma=False,
    )
```

time: 725 us -> 300 us (0.41)
  matrix products: 170 us -> 8.68 us
  local copies, waits for them, and re-layouts: 147 us -> 15.2 us
  other arithmetic: 123 us -> 5.96 us
  Pallas kernels: 0 us -> 62.2 us
  blocking collectives: 158 us -> 113 us
  starting transfers between devices: 36.2 us -> 10.2 us
  loops' own time: 9.72 us -> 0 us
  waiting for transfers between devices: 74.5 us -> 82.6 us
    dot_general x20 -> x2, matrix products: 170 us -> 8.68 us  [the longest x1 6.39 us: shards(): jnp.dot(hit.astype(jnp.bfloat16), wide, preferred_element_type=jnp.float32)]
    eq x8 -> x0, other arithmetic: 74.8 us -> none  [code_one_hot(): marked = code_block[:, :, None, :] == levels[None, None, :, None]]
    psum x1, blocking collectives: 158 us -> 92 us  [shards(): raw = lax.psum(raw, axes)]
    pallas_call x0 -> x2, Pallas kernels: none -> 62.2 us  [the longest x1 39.3 us: shards(): pl.pallas_call(grad_kernel, out_shape=(jax.ShapeDtypeStruct((lists, slots...]
    reduce_sum x13 -> x4, other arithmetic: 34.7 us -> 3.83 us  [the longest x1 1.77 us: shards(): jnp.sum(jnp.where(hit, back_top[:, None], 0.0), axis=0)]
    eq x30 -> x1, local copies, waits for them, and re-layouts: 29.4 us -> 0.01 us  [shards(): targets[None] // PASSAGES]
    all_to_all x7 -> x2, starting transfers between devices: 36.2 us -> 10.2 us  [swap(): lax.all_to_all(x, axes, split_axis=axis, concat_axis=axis, tiled=True)]
    dynamic_update_slice x12 -> x0, local copies, waits for them, and re-layouts: 21.2 us -> none  [the longest x8 18.8 us: second_pass(): lax.map(grad_piece, (got_rows.reshape(groups, group_width, slot_rows, D),...]
  transfers between devices with their start and end apart: 7 -> 2, of which waited for: 4 -> 1; matrix products, arithmetic and copies ran while one was open for 5% -> 0% of each run, Pallas kernels for 0% -> 0%
where the time goes in v1:
time: 300 us; the launch traced here: 299 us
  blocking collectives  113 us (38%)
  waiting for transfers between devices  82.6 us (28%)
  Pallas kernels  62.2 us (21%)
  local copies, waits for them, and re-layouts  15.2 us (5%)
  starting transfers between devices  10.2 us (3%)
  matrix products  8.68 us (3%)
  other arithmetic  5.96 us (2%)
    psum x1, blocking collectives, shards(): raw = lax.psum(raw, axes)  92 us
    all_to_all x2, waiting for transfers between devices, swap(): lax.all_to_all(x, axes, split_axis=axis, concat_axis=axis, tiled=True)  82.6 us
    pallas_call x1, Pallas kernels, shards(): pl.pallas_call(grad_kernel, out_shape=(jax.ShapeDtypeStruct((lists, slots...  39.3 us
    pallas_call x1, Pallas kernels, shards(): pl.pallas_call(score_kernel, out_shape=(jax.ShapeDtypeStruct((lists, slot...  22.8 us
    all_to_all x2, blocking collectives, swap(): lax.all_to_all(x, axes, split_axis=axis, concat_axis=axis, tiled=True)  20.9 us
    all_to_all x2, starting transfers between devices, swap(): lax.all_to_all(x, axes, split_axis=axis, concat_axis=axis, tiled=True)  10.2 us
    unnamed x17, local copies, waits for them, and re-layouts  6.47 us
    dot_general x1, matrix products, shards(): jnp.dot(hit.astype(jnp.bfloat16), wide, preferred_element_type=jnp.float32)  6.39 us
  transfers between devices with their start and end apart: 2, of which 1 were waited for; matrix products, arithmetic and copies ran while one was open for 0% of the time, Pallas kernels for 0%

profile of v1, /device:TPU:0, one launch (start us, length us, event | category | flops | bytes accessed | tf_op | source)
XLA Modules:
  0.0 299.3 jit_solution(13765532902798129559)
XLA Ops:
  0.6 0.7 copy.53
  1.3 0.5 convert_reduce_fusion
  1.9 0.7 add_select_fusion
  2.7 0.2 copy.52
  2.9 6.4 %fusion.4 = bf16[2048,896]{1,0:T(8,128)(2,1)S(1)} fusion(s32[1024]{0:T(1024)S(1)} %fusion.37, bf16[1024,16]{1,0:T(8,128)(2,1)S(1)} %copy.52, bf16[256,768]{1,0:T(8,128)(2,1)} %param.5), kind=kOutput, calls=%fused_computation.12 | convolution fusion | flops 3773038592 | bytes 4100096 | tf_op jit(solution)/shard_map/dot_general | solution.py:146
  9.3 2.4 copy.39
  11.7 7.4 %all-to-all-start = ((bf16[8,32,8,896]{3,2,0,1:T(8,128)(2,1)}), bf16[8,32,8,896]{3,2,0,1:T(8,128)(2,1)}, u32[]{:S(2)}, u32[]{:S(2)}) async-start(bf16[8,32,8,896]{3,2,0,1:T(8,128)(2,1)} %copy.39), calls=%async_computation | async-start | bytes 7340032 | tf_op jit(solution)/shard_map/all_to_all | solution.py:151
  19.1 0.0 copy-start.3
  19.1 82.6 %all-to-all-done = bf16[8,32,8,896]{3,2,0,1:T(8,128)(2,1)} async-done(((bf16[8,32,8,896]{3,2,0,1:T(8,128)(2,1)}), bf16[8,32,8,896]{3,2,0,1:T(8,128)(2,1)}, u32[]{:S(2)}, u32[]{:S(2)}) %all-to-all-start) | async-done | bytes 3670048 | tf_op jit(solution)/shard_map/all_to_all | solution.py:151
  101.7 2.5 copy.59
  104.3 0.0 copy-start
  104.3 0.0 copy-done.3
  104.3 22.8 %scores.1 = (f32[8,256,1024]{2,1,0:T(8,128)S(1)}, f32[8,8,256]{2,1,0:T(8,128)S(1)}) custom-call(s32[1]{0:T(128)} %bitcast.1.off_ref, bf16[8,256,896]{2,1,0:T(8,128)(2,1)S(1)} %bitcast.35, s32[32,96,1024]{2,1,0:T(8,128)} %codes_ref.3, f32[16,768]{1,0:T(8,128)S(1)} %copy-done.3), custom_call_target="tpu_custom_call" | custom-call | tf_op jit(solution)/shard_map/scores/pallas_call | solution.py:163
  127.1 0.0 copy-done
  127.1 0.0 copy-start.2
  127.2 3.2 %copy-done.2 = f32[8,256,1024]{2,1,0:T(8,128)} copy-done((f32[8,256,1024]{2,1,0:T(8,128)}, f32[8,256,1024]{2,1,0:T(8,128)S(1)}, u32[]{:S(2)}) %copy-start.2) | copy-done | bytes 8388632
  130.4 0.2 reshape.190
  130.6 0.2 copy.60
  130.7 0.2 reshape.192
  130.9 10.9 %all_to_all.20 = f32[32,1,128]{2,1,0:T(1,128)S(1)} all-to-all(f32[32,1,128]{2,1,0:T(1,128)S(1)} %reshape.192), channel_id=1, replica_groups=mesh['corpus'=8,'query'=4] {'corpus','query'}, dimensions={0} | all-to-all | bytes 32768 | tf_op jit(solution)/shard_map/all_to_all | solution.py:151
  141.8 0.5 broadcast.162
  142.3 0.7 reduce
  143.0 0.2 reshape.193
  143.3 0.1 broadcast_in_dim.79
  143.4 0.1 broadcast_in_dim.76
  143.5 1.8 select_reduce_fusion.2
  145.4 0.9 select_reduce_fusion
  146.3 0.1 reshape.186
  146.5 0.1 copy.45
  146.5 9.9 %all_to_all.21 = f32[8,32,8]{2,0,1:T(8,128)S(1)} all-to-all(f32[8,32,8]{2,0,1:T(8,128)S(1)} %copy.45), channel_id=1, replica_groups=mesh['corpus'=8,'query'=4] {'corpus','query'}, dimensions={1} | all-to-all | bytes 16384 | tf_op jit(solution)/shard_map/all_to_all | solution.py:151
  156.5 0.1 reshape.191.factor_ref
  156.6 0.0 copy-start.1
  156.6 2.0 copy-done.1
  158.7 39.3 %grads.1 = (bf16[8,256,768]{2,1,0:T(8,128)(2,1)S(1)}, f32[16,768]{1,0:T(8,128)S(1)}) custom-call(s32[1]{0:T(128)} %bitcast.1.off_ref, bf16[8,256,896]{2,1,0:T(8,128)(2,1)S(1)} %bitcast.36, s32[32,96,1024]{2,1,0:T(8,128)} %codes_ref.3, f32[16,768]{1,0:T(8,128)S(1)} %copy-done.3, f32[8,256,1024]{2,1,0:T(8,128)} %copy-done.2, f32[8,1,256]{2,1,0:T(1,128)S(1)} %reshape.191.factor_ref), custom_call_target="tpu_custom_call" | custom-call | tf_op jit(solution)/shard_map/grads/pallas_call | solution.py:190
  198.0 2.1 copy.48
  200.1 2.8 all-to-all-start.3
  202.9 92.0 %psum.7 = f32[16,768]{1,0:T(8,128)S(1)} all-reduce(f32[16,768]{1,0:T(8,128)S(1)} %get-tuple-element.9), channel_id=1, replica_groups=mesh['corpus'=8,'query'=4] {'corpus','query'}, use_global_device_ids=true, to_apply=%region_6.7 | all-reduce | flops 12288 | bytes 98304 | tf_op jit(solution)/shard_map/psum | solution.py:216
  294.9 0.6 multiply_reduce_fusion
  296.2 0.6 broadcast_multiply_fusion
  296.8 0.0 all-to-all-done.3
  296.8 0.2 copy.49
  297.1 2.3 fusion.21
  (23 shorter events, 0.3 us)
Async XLA Ops:
  11.7 90.0 %all-to-all-start = ((bf16[8,32,8,896]{3,2,0,1:T(8,128)(2,1)}), bf16[8,32,8,896]{3,2,0,1:T(8,128)(2,1)}, u32[]{:S(2)}, u32[]{:S(2)}) async-start(bf16[8,32,8,896]{3,2,0,1:T(8,128)(2,1)} %copy.39), calls=%async_computation | async-start | bytes 7340032 | tf_op jit(solution)/shard_map/all_to_all | solution.py:151
  19.1 85.2 %copy-start.3 = (f32[16,768]{1,0:T(8,128)S(1)}, f32[16,768]{1,0:T(8,128)}, u32[]{:S(2)}) copy-start(f32[16,768]{1,0:T(8,128)} %cb_ref.3) | copy-start | bytes 147460
  104.3 22.9 %copy-start = (bf16[8,32,8,896]{3,2,1,0:T(8,128)(2,1)}, bf16[8,32,8,896]{3,2,1,0:T(8,128)(2,1)S(1)}, u32[]{:S(2)}) copy-start(bf16[8,32,8,896]{3,2,1,0:T(8,128)(2,1)S(1)} %copy.59) | copy-start | bytes 11010052
  127.1 3.2 %copy-start.2 = (f32[8,256,1024]{2,1,0:T(8,128)}, f32[8,256,1024]{2,1,0:T(8,128)S(1)}, u32[]{:S(2)}) copy-start(f32[8,256,1024]{2,1,0:T(8,128)S(1)} %get-tuple-element.6.exp_ref) | copy-start | bytes 25165828
  156.6 2.0 copy-start.1
  200.1 96.8 %all-to-all-start.3 = ((bf16[8,32,8,768]{3,2,0,1:T(8,128)(2,1)}), bf16[8,32,8,768]{3,2,0,1:T(8,128)(2,1)S(1)}, u32[]{:S(2)}, u32[]{:S(2)}) async-start(bf16[8,32,8,768]{3,2,0,1:T(8,128)(2,1)} %copy.48), calls=%async_computation.3 | async-start | bytes 6291456 | tf_op jit(solution)/shard_map/all_to_all | solution.py:151

commit v2 on v1

--- a/solution.py
+++ b/solution.py
@@ -20,8 +20,7 @@
 CHUNKS = D // CHUNK
 SPACES = CHUNK // SUBDIM
 COLS = SPACES * CENTROIDS
-NOTES = 128
-WIDE = D + NOTES
+PIECES = 2
 
 NT = (((1,), (1,)), ((), ()))
 TN = (((0,), (0,)), ((), ()))
@@ -92,14 +91,15 @@
         raw[...] = jnp.zeros_like(raw)
 
     slots = exp_ref.shape[1]
-    factor = jnp.broadcast_to(factor_ref[0], (128, slots)).T[:, 0:1]
-    notes = rows_ref[0, :, D:].astype(jnp.float32)
+    held = factor_ref[0]
+    held = jnp.concatenate([held, jnp.zeros((128 - held.shape[0], slots), jnp.float32)], axis=0).T
+    factor = held[:, 0:1]
+    spots = held.astype(jnp.int32) - 1
     place = lax.broadcasted_iota(jnp.int32, (slots, PASSAGES), 1)
     teacher = jnp.zeros((slots, PASSAGES), jnp.float32)
     for r in range(TARGETS):
-        spot = (notes[:, r : r + 1] - 1.0) * 256.0 + notes[:, TARGETS + r : TARGETS + r + 1]
         weight = 2.0 * (TARGETS - r) / (TARGETS * (TARGETS + 1.0))
-        teacher = jnp.where(place == spot.astype(jnp.int32), weight, teacher)
+        teacher = jnp.where(place == spots[:, r + 1 : r + 2], weight, teacher)
     grad = (exp_ref[0] * factor - teacher).astype(jnp.bfloat16)
     for c in range(CHUNKS):
         hist = dot(grad, one_hot(codes_ref, c), NT)
@@ -138,46 +138,67 @@
 
     inside = targets[None] // PASSAGES == jnp.arange(PROBES, dtype=jnp.int32)[:, None, None]
     spot = targets[None] % PASSAGES
+    hot = hit.astype(jnp.bfloat16)
     notes = jnp.concatenate(
-        [jnp.where(inside, spot // 256 + 1, 0), jnp.where(inside, spot % 256, 0)], axis=2
-    ).reshape(entries, 2 * TARGETS)
-    notes = jnp.pad(notes, ((0, 0), (0, NOTES - 2 * TARGETS))).astype(jnp.bfloat16)
-    wide = jnp.concatenate([jnp.concatenate([queries] * PROBES, axis=0), notes], axis=1)
-    sending = jnp.dot(
-        hit.astype(jnp.bfloat16), wide, preferred_element_type=jnp.float32
-    ).astype(jnp.bfloat16)
+        [jnp.where(inside, spot // 256, 0), jnp.where(inside, spot % 256, 0), inside], axis=2
+    ).reshape(entries, 3 * TARGETS)
+    notes = lax.dot_general(
+        notes.astype(jnp.bfloat16), hot, (((0,), (1,)), ((), ())),
+        preferred_element_type=jnp.float32,
+    ).reshape(3, TARGETS, slot_count)
+    notes = notes[0] * 256.0 + notes[1] + notes[2]
 
     def swap(x, axis=1):
         return lax.all_to_all(x, axes, split_axis=axis, concat_axis=axis, tiled=True)
 
-    rows = swap(sending.reshape(lists, devices, capacity, WIDE)).reshape(lists, slots, WIDE)
-
-    offset = (lax.axis_index("query") * lists).astype(jnp.int32).reshape(1)
-    rows_spec = pl.BlockSpec((1, slots, WIDE), lambda i, off: (i, 0, 0))
+    piece = lists // PIECES
+    copies = jnp.concatenate([queries] * PROBES, axis=0)
+    rows = []
+    for i in range(PIECES):
+        sending = jnp.dot(
+            hot[i * piece * slots : (i + 1) * piece * slots],
+            copies,
+            preferred_element_type=jnp.float32,
+        ).astype(jnp.bfloat16)
+        rows.append(
+            swap(sending.reshape(piece, devices, capacity, D)).reshape(piece, slots, D)
+        )
+
+    offsets = [
+        (lax.axis_index("query") * lists + i * piece).astype(jnp.int32).reshape(1)
+        for i in range(PIECES)
+    ]
+    work = 2 * piece * slots * COLS * CHUNKS * PASSAGES
+    rows_spec = pl.BlockSpec((1, slots, D), lambda i, off: (i, 0, 0))
     codes_spec = pl.BlockSpec((1, SUBSPACES, PASSAGES), lambda i, off: (off[0] + i, 0, 0))
     cb_spec = pl.BlockSpec((CENTROIDS, D), lambda i, off: (0, 0))
     exp_spec = pl.BlockSpec((1, slots, PASSAGES), lambda i, off: (i, 0, 0))
     table = pltpu.VMEM((3, CHUNKS, COLS, CHUNK), jnp.bfloat16)
     params = pltpu.CompilerParams(vmem_limit_bytes=40 * 2**20)
 
-    exps, stats = pl.pallas_call(
+    scored = pl.pallas_call(
         score_kernel,
         out_shape=(
-            jax.ShapeDtypeStruct((lists, slots, PASSAGES), jnp.float32),
-            jax.ShapeDtypeStruct((lists, 8, slots), jnp.float32),
+            jax.ShapeDtypeStruct((piece, slots, PASSAGES), jnp.float32),
+            jax.ShapeDtypeStruct((piece, 8, slots), jnp.float32),
         ),
         grid_spec=pltpu.PrefetchScalarGridSpec(
             num_scalar_prefetch=1,
-            grid=(lists,),
+            grid=(piece,),
             in_specs=[rows_spec, codes_spec, cb_spec],
             out_specs=(exp_spec, pl.BlockSpec((1, 8, slots), lambda i, off: (i, 0, 0))),
             scratch_shapes=[table],
         ),
         compiler_params=params,
+        cost_estimate=pl.CostEstimate(
+            flops=2 * work, bytes_accessed=8 * piece * slots * PASSAGES, transcendentals=0
+        ),
         name="scores",
-    )(offset, rows, passage_codes, codebook)
-
-    back = swap(stats[:, :2].reshape(lists, 2, devices, capacity), 2)
+    )
+    done = [scored(offsets[i], rows[i], passage_codes, codebook) for i in range(PIECES)]
+    stats = jnp.concatenate([stat[:, :2] for _, stat in done], axis=0)
+
+    back = swap(stats.reshape(lists, 2, devices, capacity), 2)
     back_top = back[:, 0].reshape(slot_count)
     back_total = back[:, 1].reshape(slot_count)
     top = jnp.sum(jnp.where(hit, back_top[:, None], 0.0), axis=0).reshape(PROBES, query_rows)
@@ -185,23 +206,26 @@
     shrink = jnp.exp(top - jnp.max(top, axis=0))
     scale = (shrink / jnp.sum(total * shrink, axis=0)).reshape(entries)
     slot_scale = jnp.sum(jnp.where(hit, scale[None, :], 0.0), axis=1)
-    factor = swap(slot_scale.reshape(lists, devices, capacity)).reshape(lists, 1, slots)
-
-    part, raw = pl.pallas_call(
+    told = jnp.concatenate([slot_scale[None], notes], axis=0)
+    told = told.reshape(TARGETS + 1, lists, devices, capacity).transpose(1, 0, 2, 3)
+    told = swap(told, 2).reshape(lists, TARGETS + 1, slots)
+    told = jnp.pad(told, ((0, 0), (0, 7), (0, 0)))
+
+    graded = pl.pallas_call(
         grad_kernel,
         out_shape=(
-            jax.ShapeDtypeStruct((lists, slots, D), jnp.bfloat16),
+            jax.ShapeDtypeStruct((piece, slots, D), jnp.bfloat16),
             jax.ShapeDtypeStruct((CENTROIDS, D), jnp.float32),
         ),
         grid_spec=pltpu.PrefetchScalarGridSpec(
             num_scalar_prefetch=1,
-            grid=(lists,),
+            grid=(piece,),
             in_specs=[
                 rows_spec,
                 codes_spec,
                 cb_spec,
                 exp_spec,
-                pl.BlockSpec((1, 1, slots), lambda i, off: (i, 0, 0)),
+                pl.BlockSpec((1, TARGETS + 8, slots), lambda i, off: (i, 0, 0)),
             ],
             out_specs=(
                 pl.BlockSpec((1, slots, D), lambda i, off: (i, 0, 0)),
@@ -210,12 +234,28 @@
             scratch_shapes=[table, pltpu.VMEM((CHUNKS, COLS, CHUNK), jnp.float32)],
         ),
         compiler_params=params,
+        cost_estimate=pl.CostEstimate(
+            flops=4 * work, bytes_accessed=8 * piece * slots * PASSAGES, transcendentals=0
+        ),
         name="grads",
-    )(offset, rows, passage_codes, codebook, exps, factor)
+    )
+    returned, raw = [], 0.0
+    for i in range(PIECES):
+        part, raw_part = graded(
+            offsets[i],
+            rows[i],
+            passage_codes,
+            codebook,
+            done[i][0],
+            told[i * piece : (i + 1) * piece],
+        )
+        raw = raw + raw_part
+        part = swap(part.reshape(piece, devices, capacity, D))
+        returned.append(part.reshape(piece * slots, D))
 
     raw = lax.psum(raw, axes)
     step = raw * lax.rsqrt(jnp.mean(raw * raw) + EPSILON)
-    returned = swap(part.reshape(lists, devices, capacity, D)).reshape(slot_count, D)
+    returned = jnp.concatenate(returned, axis=0)
     by_query = functools.reduce(
         jnp.logical_or,
         [

time: 300 us -> 292 us (0.973)
  blocking collectives: 113 us -> 67.5 us
  local copies, waits for them, and re-layouts: 15.2 us -> 42.2 us
  starting transfers between devices: 10.2 us -> 22.1 us
  waiting for transfers between devices: 82.6 us -> 73.2 us
  other arithmetic: 5.96 us -> 11.3 us
    psum x1, blocking collectives: 92 us -> 58.2 us  [shards(): raw = lax.psum(raw, axes)]
    unnamed x17 -> x29, local copies, waits for them, and re-layouts: 6.47 us -> 18.7 us
    all_to_all x2 -> x5, starting transfers between devices: 10.2 us -> 22.1 us  [swap(): lax.all_to_all(x, axes, split_axis=axis, concat_axis=axis, tiled=True)]
    all_to_all x2 -> x1, blocking collectives: 20.9 us -> 9.3 us  [swap(): lax.all_to_all(x, axes, split_axis=axis, concat_axis=axis, tiled=True)]
    all_to_all x2 -> x5, waiting for transfers between devices: 82.6 us -> 73.2 us  [swap(): lax.all_to_all(x, axes, split_axis=axis, concat_axis=axis, tiled=True)]
    reshape x7 -> x8, local copies, waits for them, and re-layouts: 5.09 us -> 12.4 us  [the longest x2 5.9 us: shards(): told = swap(told, 2).reshape(lists, TARGETS + 1, slots)]
    transpose x0 -> x1, local copies, waits for them, and re-layouts: none -> 3.79 us  [shards(): told.reshape(TARGETS + 1, lists, devices, capacity).transpose(1, 0, 2, 3)]
    pallas_call x2 -> x4, Pallas kernels: 62.2 us -> 63.2 us  [the longest x2 39.4 us: shards(): graded(offsets[i], rows[i], passage_codes, codebook, done[i][0], told[i *...]
  transfers between devices with their start and end apart: 2 -> 5, of which waited for: 1 -> 4; matrix products, arithmetic and copies ran while one was open for 0% -> 5% of each run, Pallas kernels for 0% -> 11%
where the time goes in v2:
time: 292 us; the launch traced here: 291 us
  waiting for transfers between devices  73.2 us (25%)
  blocking collectives  67.5 us (23%)
  Pallas kernels  63.2 us (22%)
  local copies, waits for them, and re-layouts  42.2 us (14%)
  starting transfers between devices  22.1 us (8%)
  other arithmetic  11.3 us (4%)
  matrix products  9.41 us (3%)
    all_to_all x5, waiting for transfers between devices, swap(): lax.all_to_all(x, axes, split_axis=axis, concat_axis=axis, tiled=True)  73.2 us
    psum x1, blocking collectives, shards(): raw = lax.psum(raw, axes)  58.2 us
    pallas_call x2, Pallas kernels, shards(): graded(offsets[i], rows[i], passage_codes, codebook, done[i][0], told[i *...  39.4 us
    pallas_call x2, Pallas kernels, shards(): scored(offsets[i], rows[i], passage_codes, codebook)  23.8 us
    all_to_all x5, starting transfers between devices, swap(): lax.all_to_all(x, axes, split_axis=axis, concat_axis=axis, tiled=True)  22.1 us
    unnamed x29, local copies, waits for them, and re-layouts  18.7 us
    all_to_all x1, blocking collectives, swap(): lax.all_to_all(x, axes, split_axis=axis, concat_axis=axis, tiled=True)  9.3 us
    reshape x2, local copies, waits for them, and re-layouts, shards(): told = swap(told, 2).reshape(lists, TARGETS + 1, slots)  5.9 us
  transfers between devices with their start and end apart: 5, of which 4 were waited for; matrix products, arithmetic and copies ran while one was open for 5% of the time, Pallas kernels for 11%

profile of v2, /device:TPU:0, one launch (start us, length us, event | category | flops | bytes accessed | tf_op | source)
XLA Modules:
  0.0 290.6 jit_solution(11455798274527494960)
XLA Ops:
  0.6 0.7 copy.67
  1.9 1.0 constant_dynamic-update-slice_fusion.3
  3.0 1.0 constant_dynamic-update-slice_fusion.2
  4.0 1.0 constant_dynamic-update-slice_fusion.1
  5.1 1.8 iota_compare_fusion
  6.9 2.0 fusion.15
  8.8 1.4 copy.48
  10.2 7.3 %all-to-all-start = ((bf16[4,32,8,768]{3,2,0,1:T(8,128)(2,1)}), bf16[4,32,8,768]{3,2,0,1:T(8,128)(2,1)S(1)}, u32[]{:S(2)}, u32[]{:S(2)}) async-start(bf16[4,32,8,768]{3,2,0,1:T(8,128)(2,1)} %copy.48), calls=%async_computation | async-start | bytes 3145728 | tf_op jit(solution)/shard_map/all_to_all | solution.py:152
  17.5 3.0 %fusion.18 = bf16[1024,768]{1,0:T(8,128)(2,1)S(1)} fusion(bf16[1024,768]{1,0:T(8,128)(2,1)S(1)} %constant_dynamic-update-slice_fusion, pred[2048,1024]{1,0:T(32,128)(4,1)} %copy-done.6), kind=kOutput, calls=%fused_computation.25 | convolution fusion | flops 1611399168 | bytes 4194304 | tf_op jit(solution)/shard_map/dot_general | solution.py:158
  20.5 1.4 copy.50
  21.8 33.4 %all-to-all-done = bf16[4,32,8,768]{3,2,0,1:T(8,128)(2,1)S(1)} async-done(((bf16[4,32,8,768]{3,2,0,1:T(8,128)(2,1)}), bf16[4,32,8,768]{3,2,0,1:T(8,128)(2,1)S(1)}, u32[]{:S(2)}, u32[]{:S(2)}) %all-to-all-start) | async-done | bytes 1572896 | tf_op jit(solution)/shard_map/all_to_all | solution.py:152
  55.2 4.1 %all-to-all-start.1 = ((bf16[4,32,8,768]{3,2,0,1:T(8,128)(2,1)}), bf16[4,32,8,768]{3,2,0,1:T(8,128)(2,1)}, u32[]{:S(2)}, u32[]{:S(2)}) async-start(bf16[4,32,8,768]{3,2,0,1:T(8,128)(2,1)} %copy.50), calls=%async_computation.1 | async-start | bytes 3145728 | tf_op jit(solution)/shard_map/all_to_all | solution.py:152
  59.5 2.2 fusion
  62.4 11.9 %scores.2 = (f32[4,256,1024]{2,1,0:T(8,128)S(1)}, f32[4,8,256]{2,1,0:T(8,128)S(1)}) custom-call(s32[1]{0:T(128)} %bitcast.1.off_ref, bf16[4,256,768]{2,1,0:T(8,128)(2,1)S(1)} %bitcast.49, s32[32,96,1024]{2,1,0:T(8,128)} %codes_ref.7, f32[16,768]{1,0:T(8,128)S(1)} %copy-done), custom_call_target="tpu_custom_call" | custom-call | flops 6442450944 | bytes 8388608 | tf_op jit(solution)/shard_map/scores/pallas_call | solution.py:198
  74.3 1.9 copy-done.1
  76.3 20.6 %all-to-all-done.1 = bf16[4,32,8,768]{3,2,0,1:T(8,128)(2,1)} async-done(((bf16[4,32,8,768]{3,2,0,1:T(8,128)(2,1)}), bf16[4,32,8,768]{3,2,0,1:T(8,128)(2,1)}, u32[]{:S(2)}, u32[]{:S(2)}) %all-to-all-start.1) | async-done | bytes 1572896 | tf_op jit(solution)/shard_map/all_to_all | solution.py:152
  96.9 1.5 copy.74
  98.4 11.9 %scores.3 = (f32[4,256,1024]{2,1,0:T(8,128)S(1)}, f32[4,8,256]{2,1,0:T(8,128)S(1)}) custom-call(s32[1]{0:T(128)} %bitcast.4.off_ref, bf16[4,256,768]{2,1,0:T(8,128)(2,1)S(1)} %bitcast.51, s32[32,96,1024]{2,1,0:T(8,128)} %codes_ref.7, f32[16,768]{1,0:T(8,128)S(1)} %copy-done), custom_call_target="tpu_custom_call" | custom-call | flops 6442450944 | bytes 8388608 | tf_op jit(solution)/shard_map/scores/pallas_call | solution.py:198
  110.3 2.0 copy-done.3
  112.5 0.9 copy.76
  113.3 1.7 reshape.228
  115.0 3.8 %all-to-all-start.2 = ((f32[32,1,128]{2,1,0:T(1,128)}), f32[32,1,128]{2,1,0:T(1,128)S(1)}, u32[]{:S(2)}, u32[]{:S(2)}) async-start(f32[32,1,128]{2,1,0:T(1,128)} %reshape.228), calls=%async_computation.2 | async-start | bytes 32768 | tf_op jit(solution)/shard_map/all_to_all | solution.py:152
  118.8 0.9 slice_add_fusion
  119.7 1.6 add.78
  121.3 4.6 %all-to-all-done.2 = f32[32,1,128]{2,1,0:T(1,128)S(1)} async-done(((f32[32,1,128]{2,1,0:T(1,128)}), f32[32,1,128]{2,1,0:T(1,128)S(1)}, u32[]{:S(2)}, u32[]{:S(2)}) %all-to-all-start.2) | async-done | bytes 16416 | tf_op jit(solution)/shard_map/all_to_all | solution.py:152
  128.0 0.9 copy.54
  129.1 1.8 select_reduce_fusion.2
  131.0 0.9 select_reduce_fusion
  132.0 2.5 maximum_bitcast_fusion
  134.5 3.8 %copy.56 = f32[8,9,32,8]{1,3,0,2:T(8,128)} copy(f32[8,9,32,8]{3,2,0,1:T(8,128)} %maximum_bitcast_fusion) | data formatting | bytes 147456 | tf_op jit(solution)/shard_map/transpose | solution.py:210
  138.3 2.0 reshape.230
  140.3 9.3 %all_to_all.30 = f32[32,1,576]{2,1,0:T(1,128)S(1)} all-to-all(f32[32,1,576]{2,1,0:T(1,128)S(1)} %reshape.230), channel_id=1, replica_groups=mesh['corpus'=8,'query'=4] {'corpus','query'}, dimensions={0} | all-to-all | bytes 147456 | tf_op jit(solution)/shard_map/all_to_all | solution.py:152
  149.6 0.8 reduce.1
  150.4 2.0 reshape.231
  152.5 3.9 %copy.65 = f32[8,9,32,8]{3,2,1,0:T(8,128)} copy(f32[8,9,32,8]{1,3,0,2:T(8,128)} %bitcast.56) | data formatting | bytes 147456 | tf_op jit(solution)/shard_map/reshape | solution.py:211
  156.4 2.0 reshape.227
  158.4 2.2 copy-done.4
  160.6 19.7 %grads.3 = (bf16[4,256,768]{2,1,0:T(8,128)(2,1)S(1)}, f32[16,768]{1,0:T(8,128)S(1)}) custom-call(s32[1]{0:T(128)} %bitcast.4.off_ref, bf16[4,256,768]{2,1,0:T(8,128)(2,1)S(1)} %bitcast.52, s32[32,96,1024]{2,1,0:T(8,128)} %codes_ref.7, f32[16,768]{1,0:T(8,128)S(1)} %copy-done, f32[4,256,1024]{2,1,0:T(8,128)S(1)} %copy-done.4, ...), custom_call_target="tpu_custom_call" | custom-call | flops 12884901888 | bytes 8388608 | tf_op jit(solution)/shard_map/grads/pallas_call | solution.py:244
  180.3 1.4 copy.61
  181.7 3.4 %all-to-all-start.5 = ((bf16[4,32,8,768]{3,2,0,1:T(8,128)(2,1)}), bf16[4,32,8,768]{3,2,0,1:T(8,128)(2,1)}, u32[]{:S(2)}, u32[]{:S(2)}) async-start(bf16[4,32,8,768]{3,2,0,1:T(8,128)(2,1)} %copy.61), calls=%async_computation.5 | async-start | bytes 3145728 | tf_op jit(solution)/shard_map/all_to_all | solution.py:152
  185.1 2.2 copy-done.2
  187.3 19.7 %grads.2 = (bf16[4,256,768]{2,1,0:T(8,128)(2,1)S(1)}, f32[16,768]{1,0:T(8,128)S(1)}) custom-call(s32[1]{0:T(128)} %bitcast.1.off_ref, bf16[4,256,768]{2,1,0:T(8,128)(2,1)S(1)} %bitcast.50, s32[32,96,1024]{2,1,0:T(8,128)} %codes_ref.7, f32[16,768]{1,0:T(8,128)S(1)} %copy-done, f32[4,256,1024]{2,1,0:T(8,128)S(1)} %copy-done.2, ...), custom_call_target="tpu_custom_call" | custom-call | flops 12884901888 | bytes 8388608 | tf_op jit(solution)/shard_map/grads/pallas_call | solution.py:244
  207.0 1.4 copy.59
  208.4 14.6 %all-to-all-done.5 = bf16[4,32,8,768]{3,2,0,1:T(8,128)(2,1)} async-done(((bf16[4,32,8,768]{3,2,0,1:T(8,128)(2,1)}), bf16[4,32,8,768]{3,2,0,1:T(8,128)(2,1)}, u32[]{:S(2)}, u32[]{:S(2)}) %all-to-all-start.5) | async-done | bytes 1572896 | tf_op jit(solution)/shard_map/all_to_all | solution.py:152
  223.0 3.6 %all-to-all-start.4 = ((bf16[4,32,8,768]{3,2,0,1:T(8,128)(2,1)}), bf16[4,32,8,768]{3,2,0,1:T(8,128)(2,1)S(1)}, u32[]{:S(2)}, u32[]{:S(2)}) async-start(bf16[4,32,8,768]{3,2,0,1:T(8,128)(2,1)} %copy.59), calls=%async_computation.4 | async-start | bytes 3145728 | tf_op jit(solution)/shard_map/all_to_all | solution.py:152
  226.5 58.2 %psum.7 = f32[16,768]{1,0:T(8,128)S(1)} all-reduce(f32[16,768]{1,0:T(8,128)S(1)} %add.79), channel_id=1, replica_groups=mesh['corpus'=8,'query'=4] {'corpus','query'}, use_global_device_ids=true, to_apply=%region_6.7 | all-reduce | flops 12288 | bytes 98304 | tf_op jit(solution)/shard_map/psum | solution.py:256
  286.6 1.5 copy.62
  288.3 2.3 fusion.21
  (52 shorter events, 5.4 us)
Async XLA Ops:
  0.6 4.4 %copy-start.5 = (bf16[256,768]{1,0:T(8,128)(2,1)S(1)}, bf16[256,768]{1,0:T(8,128)(2,1)}, u32[]{:S(2)}) copy-start(bf16[256,768]{1,0:T(8,128)(2,1)} %param.5) | copy-start | bytes 1179652
  6.8 2.0 copy-start.6
  10.2 45.0 %all-to-all-start = ((bf16[4,32,8,768]{3,2,0,1:T(8,128)(2,1)}), bf16[4,32,8,768]{3,2,0,1:T(8,128)(2,1)S(1)}, u32[]{:S(2)}, u32[]{:S(2)}) async-start(bf16[4,32,8,768]{3,2,0,1:T(8,128)(2,1)} %copy.48), calls=%async_computation | async-start | bytes 3145728 | tf_op jit(solution)/shard_map/all_to_all | solution.py:152
  21.8 37.5 %copy-start.7 = (s32[256,8]{0,1:T(8,128)S(1)}, s32[256,8]{0,1:T(8,128)}, u32[]{:S(2)}) copy-start(s32[256,8]{0,1:T(8,128)} %param.7) | copy-start | bytes 24580
  55.2 41.7 %all-to-all-start.1 = ((bf16[4,32,8,768]{3,2,0,1:T(8,128)(2,1)}), bf16[4,32,8,768]{3,2,0,1:T(8,128)(2,1)}, u32[]{:S(2)}, u32[]{:S(2)}) async-start(bf16[4,32,8,768]{3,2,0,1:T(8,128)(2,1)} %copy.50), calls=%async_computation.1 | async-start | bytes 3145728 | tf_op jit(solution)/shard_map/all_to_all | solution.py:152
  61.6 0.8 copy-start
  74.3 1.9 copy-start.1
  110.3 2.0 copy-start.3
  115.0 10.8 %all-to-all-start.2 = ((f32[32,1,128]{2,1,0:T(1,128)}), f32[32,1,128]{2,1,0:T(1,128)S(1)}, u32[]{:S(2)}, u32[]{:S(2)}) async-start(f32[32,1,128]{2,1,0:T(1,128)} %reshape.228), calls=%async_computation.2 | async-start | bytes 32768 | tf_op jit(solution)/shard_map/all_to_all | solution.py:152
  158.4 2.2 copy-start.4
  181.7 41.3 %all-to-all-start.5 = ((bf16[4,32,8,768]{3,2,0,1:T(8,128)(2,1)}), bf16[4,32,8,768]{3,2,0,1:T(8,128)(2,1)}, u32[]{:S(2)}, u32[]{:S(2)}) async-start(bf16[4,32,8,768]{3,2,0,1:T(8,128)(2,1)} %copy.61), calls=%async_computation.5 | async-start | bytes 3145728 | tf_op jit(solution)/shard_map/all_to_all | solution.py:152
  185.1 2.2 copy-start.2
  223.0 65.2 %all-to-all-start.4 = ((bf16[4,32,8,768]{3,2,0,1:T(8,128)(2,1)}), bf16[4,32,8,768]{3,2,0,1:T(8,128)(2,1)S(1)}, u32[]{:S(2)}, u32[]{:S(2)}) async-start(bf16[4,32,8,768]{3,2,0,1:T(8,128)(2,1)} %copy.59), calls=%async_computation.4 | async-start | bytes 3145728 | tf_op jit(solution)/shard_map/all_to_all | solution.py:152

commit v3 on v2

--- a/solution.py
+++ b/solution.py
@@ -81,7 +81,7 @@
 
 
 def grad_kernel(
-    off_ref, rows_ref, codes_ref, cb_ref, exp_ref, factor_ref, part_ref, raw_ref, table, raw
+    off_ref, rows_ref, codes_ref, cb_ref, exp_ref, factor_ref, notes_ref, part_ref, raw_ref, table, raw
 ):
     step = pl.program_id(0)
 
@@ -91,15 +91,15 @@
         raw[...] = jnp.zeros_like(raw)
 
     slots = exp_ref.shape[1]
-    held = factor_ref[0]
-    held = jnp.concatenate([held, jnp.zeros((128 - held.shape[0], slots), jnp.float32)], axis=0).T
-    factor = held[:, 0:1]
-    spots = held.astype(jnp.int32) - 1
+    factor = jnp.broadcast_to(factor_ref[0], (128, slots)).T[:, 0:1]
+    notes = notes_ref[0]
+    notes = jnp.concatenate([notes, jnp.zeros((128 - TARGETS, slots), jnp.float32)], axis=0).T
+    spots = notes.astype(jnp.int32) - 1
     place = lax.broadcasted_iota(jnp.int32, (slots, PASSAGES), 1)
     teacher = jnp.zeros((slots, PASSAGES), jnp.float32)
     for r in range(TARGETS):
         weight = 2.0 * (TARGETS - r) / (TARGETS * (TARGETS + 1.0))
-        teacher = jnp.where(place == spots[:, r + 1 : r + 2], weight, teacher)
+        teacher = jnp.where(place == spots[:, r : r + 1], weight, teacher)
     grad = (exp_ref[0] * factor - teacher).astype(jnp.bfloat16)
     for c in range(CHUNKS):
         hist = dot(grad, one_hot(codes_ref, c), NT)
@@ -164,6 +164,9 @@
             swap(sending.reshape(piece, devices, capacity, D)).reshape(piece, slots, D)
         )
 
+    notes = swap(notes.reshape(TARGETS, lists, devices, capacity), 2)
+    notes = notes.reshape(TARGETS, lists, slots).transpose(1, 0, 2)
+
     offsets = [
         (lax.axis_index("query") * lists + i * piece).astype(jnp.int32).reshape(1)
         for i in range(PIECES)
@@ -206,10 +209,7 @@
     shrink = jnp.exp(top - jnp.max(top, axis=0))
     scale = (shrink / jnp.sum(total * shrink, axis=0)).reshape(entries)
     slot_scale = jnp.sum(jnp.where(hit, scale[None, :], 0.0), axis=1)
-    told = jnp.concatenate([slot_scale[None], notes], axis=0)
-    told = told.reshape(TARGETS + 1, lists, devices, capacity).transpose(1, 0, 2, 3)
-    told = swap(told, 2).reshape(lists, TARGETS + 1, slots)
-    told = jnp.pad(told, ((0, 0), (0, 7), (0, 0)))
+    factor = swap(slot_scale.reshape(lists, devices, capacity)).reshape(lists, 1, slots)
 
     graded = pl.pallas_call(
         grad_kernel,
@@ -225,7 +225,8 @@
                 codes_spec,
                 cb_spec,
                 exp_spec,
-                pl.BlockSpec((1, TARGETS + 8, slots), lambda i, off: (i, 0, 0)),
+                pl.BlockSpec((1, 1, slots), lambda i, off: (i, 0, 0)),
+                pl.BlockSpec((1, TARGETS, slots), lambda i, off: (i, 0, 0)),
             ],
             out_specs=(
                 pl.BlockSpec((1, slots, D), lambda i, off: (i, 0, 0)),
@@ -247,7 +248,8 @@
             passage_codes,
             codebook,
             done[i][0],
-            told[i * piece : (i + 1) * piece],
+            factor[i * piece : (i + 1) * piece],
+            notes[i * piece : (i + 1) * piece],
         )
         raw = raw + raw_part
         part = swap(part.reshape(piece, devices, capacity, D))

time: 292 us -> 286 us (0.979)
  starting transfers between devices: 22.1 us -> 33.7 us
  blocking collectives: 67.5 us -> 58.2 us
  local copies, waits for them, and re-layouts: 42.2 us -> 37.9 us
  other arithmetic: 11.3 us -> 7.88 us
    all_to_all x5 -> x7, starting transfers between devices: 22.1 us -> 33.7 us  [swap(): lax.all_to_all(x, axes, split_axis=axis, concat_axis=axis, tiled=True)]
    all_to_all x1 -> x0, blocking collectives: 9.3 us -> none  [swap(): lax.all_to_all(x, axes, split_axis=axis, concat_axis=axis, tiled=True)]
    transpose x1 -> x0, local copies, waits for them, and re-layouts: 3.79 us -> none  [shards(): told.reshape(TARGETS + 1, lists, devices, capacity).transpose(1, 0, 2, 3)]
    reshape x2 -> x4, local copies, waits for them, and re-layouts: 5.9 us -> 5.37 us  [the longest x2 4.54 us: shards(): notes = notes.reshape(TARGETS, lists, slots).transpose(1, 0, 2)]
    all_to_all x5 -> x7, waiting for transfers between devices: 73.2 us -> 73.5 us  [swap(): lax.all_to_all(x, axes, split_axis=axis, concat_axis=axis, tiled=True)]
  transfers between devices with their start and end apart: 5 -> 7, of which waited for: 4 -> 4; matrix products, arithmetic and copies ran while one was open for 5% -> 9% of each run, Pallas kernels for 11% -> 15%
where the time goes in v3:
time: 286 us; the launch traced here: 285 us
  waiting for transfers between devices  73.5 us (26%)
  Pallas kernels  63.2 us (22%)
  blocking collectives  58.2 us (20%)
  local copies, waits for them, and re-layouts  37.9 us (13%)
  starting transfers between devices  33.7 us (12%)
  matrix products  8.73 us (3%)
  other arithmetic  7.88 us (3%)
    all_to_all x7, waiting for transfers between devices, swap(): lax.all_to_all(x, axes, split_axis=axis, concat_axis=axis, tiled=True)  73.5 us
    psum x1, blocking collectives, shards(): raw = lax.psum(raw, axes)  58.2 us
    pallas_call x2, Pallas kernels, shards(): graded(offsets[i], rows[i], passage_codes, codebook, done[i][0], factor[i...  39.4 us
    all_to_all x7, starting transfers between devices, swap(): lax.all_to_all(x, axes, split_axis=axis, concat_axis=axis, tiled=True)  33.7 us
    pallas_call x2, Pallas kernels, shards(): scored(offsets[i], rows[i], passage_codes, codebook)  23.8 us
    unnamed x29, local copies, waits for them, and re-layouts  18 us
  transfers between devices with their start and end apart: 7, of which 4 were waited for; matrix products, arithmetic and copies ran while one was open for 9% of the time, Pallas kernels for 15%

profile of v3, /device:TPU:0, one launch (start us, length us, event | category | flops | bytes accessed | tf_op | source)
XLA Modules:
  0.0 284.9 jit_solution(12711840502389055376)
XLA Ops:
  0.6 0.7 copy.80
  1.9 1.0 constant_dynamic-update-slice_fusion.3
  3.0 1.0 constant_dynamic-update-slice_fusion.2
  4.0 1.0 constant_dynamic-update-slice_fusion.1
  5.1 1.8 iota_compare_fusion
  6.9 2.0 fusion.15
  8.8 1.3 copy.56
  10.2 7.3 %all-to-all-start = ((bf16[4,32,8,768]{3,2,0,1:T(8,128)(2,1)}), bf16[4,32,8,768]{3,2,0,1:T(8,128)(2,1)S(1)}, u32[]{:S(2)}, u32[]{:S(2)}) async-start(bf16[4,32,8,768]{3,2,0,1:T(8,128)(2,1)} %copy.56), calls=%async_computation | async-start | bytes 3145728 | tf_op jit(solution)/shard_map/all_to_all | solution.py:152
  17.5 3.0 %fusion.18 = bf16[1024,768]{1,0:T(8,128)(2,1)S(1)} fusion(bf16[1024,768]{1,0:T(8,128)(2,1)S(1)} %constant_dynamic-update-slice_fusion, pred[2048,1024]{1,0:T(32,128)(4,1)} %copy-done.6), kind=kOutput, calls=%fused_computation.25 | convolution fusion | flops 1611399168 | bytes 4194304 | tf_op jit(solution)/shard_map/dot_general | solution.py:158
  20.5 1.4 copy.58
  21.8 33.4 %all-to-all-done = bf16[4,32,8,768]{3,2,0,1:T(8,128)(2,1)S(1)} async-done(((bf16[4,32,8,768]{3,2,0,1:T(8,128)(2,1)}), bf16[4,32,8,768]{3,2,0,1:T(8,128)(2,1)S(1)}, u32[]{:S(2)}, u32[]{:S(2)}) %all-to-all-start) | async-done | bytes 1572896 | tf_op jit(solution)/shard_map/all_to_all | solution.py:152
  55.2 3.9 %all-to-all-start.1 = ((bf16[4,32,8,768]{3,2,0,1:T(8,128)(2,1)}), bf16[4,32,8,768]{3,2,0,1:T(8,128)(2,1)}, u32[]{:S(2)}, u32[]{:S(2)}) async-start(bf16[4,32,8,768]{3,2,0,1:T(8,128)(2,1)} %copy.58), calls=%async_computation.1 | async-start | bytes 3145728 | tf_op jit(solution)/shard_map/all_to_all | solution.py:152
  59.3 1.5 fusion
  61.3 1.6 copy.90
  62.9 2.4 reshape.234
  65.4 11.9 %scores.2 = (f32[4,256,1024]{2,1,0:T(8,128)S(1)}, f32[4,8,256]{2,1,0:T(8,128)S(1)}) custom-call(s32[1]{0:T(128)} %bitcast.1.off_ref, bf16[4,256,768]{2,1,0:T(8,128)(2,1)S(1)} %bitcast.54, s32[32,96,1024]{2,1,0:T(8,128)} %codes_ref.7, f32[16,768]{1,0:T(8,128)S(1)} %copy-done), custom_call_target="tpu_custom_call" | custom-call | flops 6442450944 | bytes 8388608 | tf_op jit(solution)/shard_map/scores/pallas_call | solution.py:201
  77.3 2.0 copy-done.3
  79.3 17.5 %all-to-all-done.1 = bf16[4,32,8,768]{3,2,0,1:T(8,128)(2,1)} async-done(((bf16[4,32,8,768]{3,2,0,1:T(8,128)(2,1)}), bf16[4,32,8,768]{3,2,0,1:T(8,128)(2,1)}, u32[]{:S(2)}, u32[]{:S(2)}) %all-to-all-start.1) | async-done | bytes 1572896 | tf_op jit(solution)/shard_map/all_to_all | solution.py:152
  96.8 4.0 %all-to-all-start.4 = ((f32[32,1,512]{2,1,0:T(1,128)}), f32[32,1,512]{2,1,0:T(1,128)S(1)}, u32[]{:S(2)}, u32[]{:S(2)}) async-start(f32[32,1,512]{2,1,0:T(1,128)} %reshape.234), calls=%async_computation.4 | async-start | bytes 131072 | tf_op jit(solution)/shard_map/all_to_all | solution.py:152
  100.8 1.5 copy.88
  102.3 11.9 %scores.3 = (f32[4,256,1024]{2,1,0:T(8,128)S(1)}, f32[4,8,256]{2,1,0:T(8,128)S(1)}) custom-call(s32[1]{0:T(128)} %bitcast.4.off_ref, bf16[4,256,768]{2,1,0:T(8,128)(2,1)S(1)} %bitcast.52, s32[32,96,1024]{2,1,0:T(8,128)} %codes_ref.7, f32[16,768]{1,0:T(8,128)S(1)} %copy-done), custom_call_target="tpu_custom_call" | custom-call | flops 6442450944 | bytes 8388608 | tf_op jit(solution)/shard_map/scores/pallas_call | solution.py:201
  114.2 1.9 copy-done.1
  116.4 0.9 copy.91
  117.2 1.7 reshape.232
  118.9 5.7 %all-to-all-start.2 = ((f32[32,1,128]{2,1,0:T(1,128)}), f32[32,1,128]{2,1,0:T(1,128)S(1)}, u32[]{:S(2)}, u32[]{:S(2)}) async-start(f32[32,1,128]{2,1,0:T(1,128)} %reshape.232), calls=%async_computation.2 | async-start | bytes 32768 | tf_op jit(solution)/shard_map/all_to_all | solution.py:152
  125.1 0.8 reduce.1
  125.9 1.6 reshape.235
  127.6 2.8 copy.78
  130.3 1.8 reshape.231
  132.1 0.7 reduce
  133.8 0.9 copy.62
  134.8 1.8 select_reduce_fusion.2
  136.7 0.9 select_reduce_fusion
  137.8 0.7 copy.64
  138.5 5.8 %all-to-all-start.3 = ((f32[8,32,8]{2,0,1:T(8,128)}), f32[8,32,8]{2,0,1:T(8,128)S(1)}, u32[]{:S(2)}, u32[]{:S(2)}) async-start(f32[8,32,8]{2,0,1:T(8,128)} %copy.64), calls=%async_computation.3 | async-start | bytes 262144 | tf_op jit(solution)/shard_map/all_to_all | solution.py:152
  144.3 8.2 %all-to-all-done.3 = f32[8,32,8]{2,0,1:T(8,128)S(1)} async-done(((f32[8,32,8]{2,0,1:T(8,128)}), f32[8,32,8]{2,0,1:T(8,128)S(1)}, u32[]{:S(2)}, u32[]{:S(2)}) %all-to-all-start.3) | async-done | bytes 8224 | tf_op jit(solution)/shard_map/all_to_all | solution.py:152
  152.7 2.2 copy-done.4
  154.9 19.7 %grads.2 = (bf16[4,256,768]{2,1,0:T(8,128)(2,1)S(1)}, f32[16,768]{1,0:T(8,128)S(1)}) custom-call(s32[1]{0:T(128)} %bitcast.1.off_ref, bf16[4,256,768]{2,1,0:T(8,128)(2,1)S(1)} %bitcast.55, s32[32,96,1024]{2,1,0:T(8,128)} %codes_ref.7, f32[16,768]{1,0:T(8,128)S(1)} %copy-done, f32[4,256,1024]{2,1,0:T(8,128)S(1)} %copy-done.4, ...), custom_call_target="tpu_custom_call" | custom-call | flops 12884901888 | bytes 8388608 | tf_op jit(solution)/shard_map/grads/pallas_call | solution.py:245
  174.6 1.4 copy.70
  176.0 3.6 %all-to-all-start.5 = ((bf16[4,32,8,768]{3,2,0,1:T(8,128)(2,1)}), bf16[4,32,8,768]{3,2,0,1:T(8,128)(2,1)}, u32[]{:S(2)}, u32[]{:S(2)}) async-start(bf16[4,32,8,768]{3,2,0,1:T(8,128)(2,1)} %copy.70), calls=%async_computation.5 | async-start | bytes 3145728 | tf_op jit(solution)/shard_map/all_to_all | solution.py:152
  179.8 2.2 copy-done.2
  181.9 19.7 %grads.3 = (bf16[4,256,768]{2,1,0:T(8,128)(2,1)S(1)}, f32[16,768]{1,0:T(8,128)S(1)}) custom-call(s32[1]{0:T(128)} %bitcast.4.off_ref, bf16[4,256,768]{2,1,0:T(8,128)(2,1)S(1)} %bitcast.53, s32[32,96,1024]{2,1,0:T(8,128)} %codes_ref.7, f32[16,768]{1,0:T(8,128)S(1)} %copy-done, f32[4,256,1024]{2,1,0:T(8,128)S(1)} %copy-done.2, ...), custom_call_target="tpu_custom_call" | custom-call | flops 12884901888 | bytes 8388608 | tf_op jit(solution)/shard_map/grads/pallas_call | solution.py:245
  201.7 1.4 copy.74
  203.0 14.3 %all-to-all-done.5 = bf16[4,32,8,768]{3,2,0,1:T(8,128)(2,1)} async-done(((bf16[4,32,8,768]{3,2,0,1:T(8,128)(2,1)}), bf16[4,32,8,768]{3,2,0,1:T(8,128)(2,1)}, u32[]{:S(2)}, u32[]{:S(2)}) %all-to-all-start.5) | async-done | bytes 1572896 | tf_op jit(solution)/shard_map/all_to_all | solution.py:152
  217.4 3.4 %all-to-all-start.6 = ((bf16[4,32,8,768]{3,2,0,1:T(8,128)(2,1)}), bf16[4,32,8,768]{3,2,0,1:T(8,128)(2,1)S(1)}, u32[]{:S(2)}, u32[]{:S(2)}) async-start(bf16[4,32,8,768]{3,2,0,1:T(8,128)(2,1)} %copy.74), calls=%async_computation.6 | async-start | bytes 3145728 | tf_op jit(solution)/shard_map/all_to_all | solution.py:152
  220.8 58.2 %psum.7 = f32[16,768]{1,0:T(8,128)S(1)} all-reduce(f32[16,768]{1,0:T(8,128)S(1)} %add.77), channel_id=1, replica_groups=mesh['corpus'=8,'query'=4] {'corpus','query'}, use_global_device_ids=true, to_apply=%region_6.7 | all-reduce | flops 12288 | bytes 98304 | tf_op jit(solution)/shard_map/psum | solution.py:258
  280.9 1.5 copy.71
  282.6 2.3 fusion.21
  (60 shorter events, 4.9 us)
Async XLA Ops:
  0.6 4.4 %copy-start.5 = (bf16[256,768]{1,0:T(8,128)(2,1)S(1)}, bf16[256,768]{1,0:T(8,128)(2,1)}, u32[]{:S(2)}) copy-start(bf16[256,768]{1,0:T(8,128)(2,1)} %param.5) | copy-start | bytes 1179652
  6.8 2.0 copy-start.6
  10.2 45.0 %all-to-all-start = ((bf16[4,32,8,768]{3,2,0,1:T(8,128)(2,1)}), bf16[4,32,8,768]{3,2,0,1:T(8,128)(2,1)S(1)}, u32[]{:S(2)}, u32[]{:S(2)}) async-start(bf16[4,32,8,768]{3,2,0,1:T(8,128)(2,1)} %copy.56), calls=%async_computation | async-start | bytes 3145728 | tf_op jit(solution)/shard_map/all_to_all | solution.py:152
  21.8 37.3 %copy-start.7 = (s32[256,8]{0,1:T(8,128)S(1)}, s32[256,8]{0,1:T(8,128)}, u32[]{:S(2)}) copy-start(s32[256,8]{0,1:T(8,128)} %param.7) | copy-start | bytes 24580
  55.2 41.6 %all-to-all-start.1 = ((bf16[4,32,8,768]{3,2,0,1:T(8,128)(2,1)}), bf16[4,32,8,768]{3,2,0,1:T(8,128)(2,1)}, u32[]{:S(2)}, u32[]{:S(2)}) async-start(bf16[4,32,8,768]{3,2,0,1:T(8,128)(2,1)} %copy.58), calls=%async_computation.1 | async-start | bytes 3145728 | tf_op jit(solution)/shard_map/all_to_all | solution.py:152
  62.9 2.5 copy-start
  77.3 2.0 copy-start.3
  96.8 22.1 %all-to-all-start.4 = ((f32[32,1,512]{2,1,0:T(1,128)}), f32[32,1,512]{2,1,0:T(1,128)S(1)}, u32[]{:S(2)}, u32[]{:S(2)}) async-start(f32[32,1,512]{2,1,0:T(1,128)} %reshape.234), calls=%async_computation.4 | async-start | bytes 131072 | tf_op jit(solution)/shard_map/all_to_all | solution.py:152
  114.2 2.0 copy-start.1
  118.9 13.2 %all-to-all-start.2 = ((f32[32,1,128]{2,1,0:T(1,128)}), f32[32,1,128]{2,1,0:T(1,128)S(1)}, u32[]{:S(2)}, u32[]{:S(2)}) async-start(f32[32,1,128]{2,1,0:T(1,128)} %reshape.232), calls=%async_computation.2 | async-start | bytes 32768 | tf_op jit(solution)/shard_map/all_to_all | solution.py:152
  138.5 14.1 %all-to-all-start.3 = ((f32[8,32,8]{2,0,1:T(8,128)}), f32[8,32,8]{2,0,1:T(8,128)S(1)}, u32[]{:S(2)}, u32[]{:S(2)}) async-start(f32[8,32,8]{2,0,1:T(8,128)} %copy.64), calls=%async_computation.3 | async-start | bytes 262144 | tf_op jit(solution)/shard_map/all_to_all | solution.py:152
  152.7 2.2 copy-start.4
  176.0 41.4 %all-to-all-start.5 = ((bf16[4,32,8,768]{3,2,0,1:T(8,128)(2,1)}), bf16[4,32,8,768]{3,2,0,1:T(8,128)(2,1)}, u32[]{:S(2)}, u32[]{:S(2)}) async-start(bf16[4,32,8,768]{3,2,0,1:T(8,128)(2,1)} %copy.70), calls=%async_computation.5 | async-start | bytes 3145728 | tf_op jit(solution)/shard_map/all_to_all | solution.py:152
  179.8 2.2 copy-start.2
  217.4 65.1 %all-to-all-start.6 = ((bf16[4,32,8,768]{3,2,0,1:T(8,128)(2,1)}), bf16[4,32,8,768]{3,2,0,1:T(8,128)(2,1)S(1)}, u32[]{:S(2)}, u32[]{:S(2)}) async-start(bf16[4,32,8,768]{3,2,0,1:T(8,128)(2,1)} %copy.74), calls=%async_computation.6 | async-start | bytes 3145728 | tf_op jit(solution)/shard_map/all_to_all | solution.py:152

commit v4 on v3

--- a/solution.py
+++ b/solution.py
@@ -252,10 +252,11 @@
             notes[i * piece : (i + 1) * piece],
         )
         raw = raw + raw_part
+        if i == PIECES - 1:
+            part, raw = lax.optimization_barrier((part, lax.psum(raw, axes)))
         part = swap(part.reshape(piece, devices, capacity, D))
         returned.append(part.reshape(piece * slots, D))
 
-    raw = lax.psum(raw, axes)
     step = raw * lax.rsqrt(jnp.mean(raw * raw) + EPSILON)
     returned = jnp.concatenate(returned, axis=0)
     by_query = functools.reduce(

time: 286 us -> 290 us (1.014)
  waiting for transfers between devices: 73.5 us -> 93.4 us
  blocking collectives: 58.2 us -> 41.3 us
    all_to_all x7, waiting for transfers between devices: 73.5 us -> 93.4 us  [swap(): lax.all_to_all(x, axes, split_axis=axis, concat_axis=axis, tiled=True)]
    psum x1, blocking collectives: 58.2 us -> 41.3 us  [shards(): part, raw = lax.optimization_barrier((part, lax.psum(raw, axes)))]
where the time goes in v4:
time: 290 us; the launch traced here: 289 us
  waiting for transfers between devices  93.4 us (32%)
  Pallas kernels  63.2 us (22%)
  blocking collectives  41.3 us (14%)
  local copies, waits for them, and re-layouts  37.9 us (13%)
  starting transfers between devices  34.6 us (12%)
  matrix products  8.73 us (3%)
  other arithmetic  7.88 us (3%)
    all_to_all x7, waiting for transfers between devices, swap(): lax.all_to_all(x, axes, split_axis=axis, concat_axis=axis, tiled=True)  93.4 us
    psum x1, blocking collectives, shards(): part, raw = lax.optimization_barrier((part, lax.psum(raw, axes)))  41.3 us
    pallas_call x2, Pallas kernels, shards(): graded(offsets[i], rows[i], passage_codes, codebook, done[i][0], factor[i...  39.4 us
    all_to_all x7, starting transfers between devices, swap(): lax.all_to_all(x, axes, split_axis=axis, concat_axis=axis, tiled=True)  34.6 us
    pallas_call x2, Pallas kernels, shards(): scored(offsets[i], rows[i], passage_codes, codebook)  23.8 us
    unnamed x29, local copies, waits for them, and re-layouts  18 us
  transfers between devices with their start and end apart: 7, of which 4 were waited for; matrix products, arithmetic and copies ran while one was open for 9% of the time, Pallas kernels for 15%

profile of v4, /device:TPU:0, one launch (start us, length us, event | category | flops | bytes accessed | tf_op | source)
XLA Modules:
  0.0 288.8 jit_solution(7457404244331421516)
XLA Ops:
  0.6 0.7 copy.80
  1.9 1.0 constant_dynamic-update-slice_fusion.3
  3.0 1.0 constant_dynamic-update-slice_fusion.2
  4.0 1.0 constant_dynamic-update-slice_fusion.1
  5.1 1.8 iota_compare_fusion
  6.9 2.0 fusion.15
  8.8 1.3 copy.56
  10.2 7.3 %all-to-all-start = ((bf16[4,32,8,768]{3,2,0,1:T(8,128)(2,1)}), bf16[4,32,8,768]{3,2,0,1:T(8,128)(2,1)S(1)}, u32[]{:S(2)}, u32[]{:S(2)}) async-start(bf16[4,32,8,768]{3,2,0,1:T(8,128)(2,1)} %copy.56), calls=%async_computation | async-start | bytes 3145728 | tf_op jit(solution)/shard_map/all_to_all | solution.py:152
  17.5 3.0 %fusion.18 = bf16[1024,768]{1,0:T(8,128)(2,1)S(1)} fusion(bf16[1024,768]{1,0:T(8,128)(2,1)S(1)} %constant_dynamic-update-slice_fusion, pred[2048,1024]{1,0:T(32,128)(4,1)} %copy-done.6), kind=kOutput, calls=%fused_computation.25 | convolution fusion | flops 1611399168 | bytes 4194304 | tf_op jit(solution)/shard_map/dot_general | solution.py:158
  20.5 1.4 copy.58
  21.8 33.4 %all-to-all-done = bf16[4,32,8,768]{3,2,0,1:T(8,128)(2,1)S(1)} async-done(((bf16[4,32,8,768]{3,2,0,1:T(8,128)(2,1)}), bf16[4,32,8,768]{3,2,0,1:T(8,128)(2,1)S(1)}, u32[]{:S(2)}, u32[]{:S(2)}) %all-to-all-start) | async-done | bytes 1572896 | tf_op jit(solution)/shard_map/all_to_all | solution.py:152
  55.2 3.9 %all-to-all-start.1 = ((bf16[4,32,8,768]{3,2,0,1:T(8,128)(2,1)}), bf16[4,32,8,768]{3,2,0,1:T(8,128)(2,1)}, u32[]{:S(2)}, u32[]{:S(2)}) async-start(bf16[4,32,8,768]{3,2,0,1:T(8,128)(2,1)} %copy.58), calls=%async_computation.1 | async-start | bytes 3145728 | tf_op jit(solution)/shard_map/all_to_all | solution.py:152
  59.3 1.5 fusion
  61.3 1.6 copy.90
  62.9 2.4 reshape.234
  65.4 11.9 %scores.2 = (f32[4,256,1024]{2,1,0:T(8,128)S(1)}, f32[4,8,256]{2,1,0:T(8,128)S(1)}) custom-call(s32[1]{0:T(128)} %bitcast.1.off_ref, bf16[4,256,768]{2,1,0:T(8,128)(2,1)S(1)} %bitcast.54, s32[32,96,1024]{2,1,0:T(8,128)} %codes_ref.7, f32[16,768]{1,0:T(8,128)S(1)} %copy-done), custom_call_target="tpu_custom_call" | custom-call | flops 6442450944 | bytes 8388608 | tf_op jit(solution)/shard_map/scores/pallas_call | solution.py:201
  77.3 2.0 copy-done.3
  79.3 17.5 %all-to-all-done.1 = bf16[4,32,8,768]{3,2,0,1:T(8,128)(2,1)} async-done(((bf16[4,32,8,768]{3,2,0,1:T(8,128)(2,1)}), bf16[4,32,8,768]{3,2,0,1:T(8,128)(2,1)}, u32[]{:S(2)}, u32[]{:S(2)}) %all-to-all-start.1) | async-done | bytes 1572896 | tf_op jit(solution)/shard_map/all_to_all | solution.py:152
  96.8 4.0 %all-to-all-start.4 = ((f32[32,1,512]{2,1,0:T(1,128)}), f32[32,1,512]{2,1,0:T(1,128)S(1)}, u32[]{:S(2)}, u32[]{:S(2)}) async-start(f32[32,1,512]{2,1,0:T(1,128)} %reshape.234), calls=%async_computation.4 | async-start | bytes 131072 | tf_op jit(solution)/shard_map/all_to_all | solution.py:152
  100.8 1.5 copy.88
  102.3 11.9 %scores.3 = (f32[4,256,1024]{2,1,0:T(8,128)S(1)}, f32[4,8,256]{2,1,0:T(8,128)S(1)}) custom-call(s32[1]{0:T(128)} %bitcast.4.off_ref, bf16[4,256,768]{2,1,0:T(8,128)(2,1)S(1)} %bitcast.52, s32[32,96,1024]{2,1,0:T(8,128)} %codes_ref.7, f32[16,768]{1,0:T(8,128)S(1)} %copy-done), custom_call_target="tpu_custom_call" | custom-call | flops 6442450944 | bytes 8388608 | tf_op jit(solution)/shard_map/scores/pallas_call | solution.py:201
  114.2 1.9 copy-done.1
  116.4 0.9 copy.91
  117.2 1.7 reshape.232
  118.9 5.7 %all-to-all-start.2 = ((f32[32,1,128]{2,1,0:T(1,128)}), f32[32,1,128]{2,1,0:T(1,128)S(1)}, u32[]{:S(2)}, u32[]{:S(2)}) async-start(f32[32,1,128]{2,1,0:T(1,128)} %reshape.232), calls=%async_computation.2 | async-start | bytes 32768 | tf_op jit(solution)/shard_map/all_to_all | solution.py:152
  125.1 0.8 reduce.1
  125.9 1.6 reshape.235
  127.6 2.8 copy.78
  130.3 1.8 reshape.231
  132.1 0.7 reduce
  133.8 0.9 copy.62
  134.8 1.8 select_reduce_fusion.2
  136.7 0.9 select_reduce_fusion
  137.8 0.7 copy.64
  138.5 5.8 %all-to-all-start.3 = ((f32[8,32,8]{2,0,1:T(8,128)}), f32[8,32,8]{2,0,1:T(8,128)S(1)}, u32[]{:S(2)}, u32[]{:S(2)}) async-start(f32[8,32,8]{2,0,1:T(8,128)} %copy.64), calls=%async_computation.3 | async-start | bytes 262144 | tf_op jit(solution)/shard_map/all_to_all | solution.py:152
  144.3 8.2 %all-to-all-done.3 = f32[8,32,8]{2,0,1:T(8,128)S(1)} async-done(((f32[8,32,8]{2,0,1:T(8,128)}), f32[8,32,8]{2,0,1:T(8,128)S(1)}, u32[]{:S(2)}, u32[]{:S(2)}) %all-to-all-start.3) | async-done | bytes 8224 | tf_op jit(solution)/shard_map/all_to_all | solution.py:152
  152.7 2.2 copy-done.4
  154.9 19.7 %grads.2 = (bf16[4,256,768]{2,1,0:T(8,128)(2,1)S(1)}, f32[16,768]{1,0:T(8,128)S(1)}) custom-call(s32[1]{0:T(128)} %bitcast.1.off_ref, bf16[4,256,768]{2,1,0:T(8,128)(2,1)S(1)} %bitcast.55, s32[32,96,1024]{2,1,0:T(8,128)} %codes_ref.7, f32[16,768]{1,0:T(8,128)S(1)} %copy-done, f32[4,256,1024]{2,1,0:T(8,128)S(1)} %copy-done.4, ...), custom_call_target="tpu_custom_call" | custom-call | flops 12884901888 | bytes 8388608 | tf_op jit(solution)/shard_map/grads/pallas_call | solution.py:245
  174.6 1.4 copy.70
  176.0 3.6 %all-to-all-start.5 = ((bf16[4,32,8,768]{3,2,0,1:T(8,128)(2,1)}), bf16[4,32,8,768]{3,2,0,1:T(8,128)(2,1)}, u32[]{:S(2)}, u32[]{:S(2)}) async-start(bf16[4,32,8,768]{3,2,0,1:T(8,128)(2,1)} %copy.70), calls=%async_computation.5 | async-start | bytes 3145728 | tf_op jit(solution)/shard_map/all_to_all | solution.py:152
  179.8 2.2 copy-done.2
  181.9 19.7 %grads.3 = (bf16[4,256,768]{2,1,0:T(8,128)(2,1)S(1)}, f32[16,768]{1,0:T(8,128)S(1)}) custom-call(s32[1]{0:T(128)} %bitcast.4.off_ref, bf16[4,256,768]{2,1,0:T(8,128)(2,1)S(1)} %bitcast.53, s32[32,96,1024]{2,1,0:T(8,128)} %codes_ref.7, f32[16,768]{1,0:T(8,128)S(1)} %copy-done, f32[4,256,1024]{2,1,0:T(8,128)S(1)} %copy-done.2, ...), custom_call_target="tpu_custom_call" | custom-call | flops 12884901888 | bytes 8388608 | tf_op jit(solution)/shard_map/grads/pallas_call | solution.py:245
  201.7 41.3 %psum.7 = f32[16,768]{1,0:T(8,128)S(1)} all-reduce(f32[16,768]{1,0:T(8,128)S(1)} %add.77), channel_id=1, replica_groups=mesh['corpus'=8,'query'=4] {'corpus','query'}, use_global_device_ids=true, to_apply=%region_6.7 | all-reduce | flops 12288 | bytes 98304 | tf_op jit(solution)/shard_map/psum | solution.py:256
  242.9 1.4 copy.74
  244.3 4.4 %all-to-all-start.6 = ((bf16[4,32,8,768]{3,2,0,1:T(8,128)(2,1)}), bf16[4,32,8,768]{3,2,0,1:T(8,128)(2,1)S(1)}, u32[]{:S(2)}, u32[]{:S(2)}) async-start(bf16[4,32,8,768]{3,2,0,1:T(8,128)(2,1)} %copy.74), calls=%async_computation.6 | async-start | bytes 3145728 | tf_op jit(solution)/shard_map/all_to_all | solution.py:152
  250.6 1.5 copy.71
  252.1 34.3 %all-to-all-done.6 = bf16[4,32,8,768]{3,2,0,1:T(8,128)(2,1)S(1)} async-done(((bf16[4,32,8,768]{3,2,0,1:T(8,128)(2,1)}), bf16[4,32,8,768]{3,2,0,1:T(8,128)(2,1)S(1)}, u32[]{:S(2)}, u32[]{:S(2)}) %all-to-all-start.6) | async-done | bytes 1572896 | tf_op jit(solution)/shard_map/all_to_all | solution.py:152
  286.5 2.3 fusion.21
  (60 shorter events, 4.9 us)
Async XLA Ops:
  0.6 4.4 %copy-start.5 = (bf16[256,768]{1,0:T(8,128)(2,1)S(1)}, bf16[256,768]{1,0:T(8,128)(2,1)}, u32[]{:S(2)}) copy-start(bf16[256,768]{1,0:T(8,128)(2,1)} %param.5) | copy-start | bytes 1179652
  6.8 2.0 copy-start.6
  10.2 45.0 %all-to-all-start = ((bf16[4,32,8,768]{3,2,0,1:T(8,128)(2,1)}), bf16[4,32,8,768]{3,2,0,1:T(8,128)(2,1)S(1)}, u32[]{:S(2)}, u32[]{:S(2)}) async-start(bf16[4,32,8,768]{3,2,0,1:T(8,128)(2,1)} %copy.56), calls=%async_computation | async-start | bytes 3145728 | tf_op jit(solution)/shard_map/all_to_all | solution.py:152
  21.8 37.3 %copy-start.7 = (s32[256,8]{0,1:T(8,128)S(1)}, s32[256,8]{0,1:T(8,128)}, u32[]{:S(2)}) copy-start(s32[256,8]{0,1:T(8,128)} %param.7) | copy-start | bytes 24580
  55.2 41.6 %all-to-all-start.1 = ((bf16[4,32,8,768]{3,2,0,1:T(8,128)(2,1)}), bf16[4,32,8,768]{3,2,0,1:T(8,128)(2,1)}, u32[]{:S(2)}, u32[]{:S(2)}) async-start(bf16[4,32,8,768]{3,2,0,1:T(8,128)(2,1)} %copy.58), calls=%async_computation.1 | async-start | bytes 3145728 | tf_op jit(solution)/shard_map/all_to_all | solution.py:152
  62.9 2.5 copy-start
  77.3 2.0 copy-start.3
  96.8 22.1 %all-to-all-start.4 = ((f32[32,1,512]{2,1,0:T(1,128)}), f32[32,1,512]{2,1,0:T(1,128)S(1)}, u32[]{:S(2)}, u32[]{:S(2)}) async-start(f32[32,1,512]{2,1,0:T(1,128)} %reshape.234), calls=%async_computation.4 | async-start | bytes 131072 | tf_op jit(solution)/shard_map/all_to_all | solution.py:152
  114.2 2.0 copy-start.1
  118.9 13.2 %all-to-all-start.2 = ((f32[32,1,128]{2,1,0:T(1,128)}), f32[32,1,128]{2,1,0:T(1,128)S(1)}, u32[]{:S(2)}, u32[]{:S(2)}) async-start(f32[32,1,128]{2,1,0:T(1,128)} %reshape.232), calls=%async_computation.2 | async-start | bytes 32768 | tf_op jit(solution)/shard_map/all_to_all | solution.py:152
  138.5 14.1 %all-to-all-start.3 = ((f32[8,32,8]{2,0,1:T(8,128)}), f32[8,32,8]{2,0,1:T(8,128)S(1)}, u32[]{:S(2)}, u32[]{:S(2)}) async-start(f32[8,32,8]{2,0,1:T(8,128)} %copy.64), calls=%async_computation.3 | async-start | bytes 262144 | tf_op jit(solution)/shard_map/all_to_all | solution.py:152
  152.7 2.2 copy-start.4
  176.0 68.3 %all-to-all-start.5 = ((bf16[4,32,8,768]{3,2,0,1:T(8,128)(2,1)}), bf16[4,32,8,768]{3,2,0,1:T(8,128)(2,1)}, u32[]{:S(2)}, u32[]{:S(2)}) async-start(bf16[4,32,8,768]{3,2,0,1:T(8,128)(2,1)} %copy.70), calls=%async_computation.5 | async-start | bytes 3145728 | tf_op jit(solution)/shard_map/all_to_all | solution.py:152
  179.8 2.2 copy-start.2
  244.3 42.1 %all-to-all-start.6 = ((bf16[4,32,8,768]{3,2,0,1:T(8,128)(2,1)}), bf16[4,32,8,768]{3,2,0,1:T(8,128)(2,1)S(1)}, u32[]{:S(2)}, u32[]{:S(2)}) async-start(bf16[4,32,8,768]{3,2,0,1:T(8,128)(2,1)} %copy.74), calls=%async_computation.6 | async-start | bytes 3145728 | tf_op jit(solution)/shard_map/all_to_all | solution.py:152
